TPU v7x, 128 devices: a whole 4x4x4 slice. The times are simulated.
128 devices in a mesh: seq: 16 (over y_hi, z, core), tp: 8 (over x, y_lo).
Axes of the slice: x: 4, y: 4 (y_hi: 2, y_lo: 2; y = y_hi * 2 + y_lo), z: 4, core: 2. Of those that a mesh axis runs over, the one named last changes fastest.
Arguments:
- tokens: bfloat16 [2048, 8192], P('tp', 'seq'), may hold values from -6 to 6
- in_weight: bfloat16 [8192, 3, 8192], P('seq', None, 'tp'), may hold values from -0.0625 to 0.0625
- residues: float32 [16, 8192], P(None, 'tp'), may hold values from -0.3125 to 0.3125
- decay_rates: float32 [16, 8192], P(None, 'tp'), may hold values from 0.000146484375 to 0.05
- skip_gain: float32 [8192], P('tp'), may hold values from 0.5 to 1.5
- out_weight: bfloat16 [8192, 8192], P('tp', 'seq'), may hold values from -0.0625 to 0.0625
Outputs:
- block_output: bfloat16 [2048, 8192], P('tp', 'seq')
All inputs are finite; a program needn't handle non-finite values.
Results may differ from a plain program's by a relative error of at most 0.038.
Values may be sent and summed in bfloat16 or wider, within the bound.
A program may use at most 128 MiB of HBM per device.

v0:
```python
import math

import jax
import jax.numpy as jnp
from jax import lax
from jax.sharding import PartitionSpec as P

HIGHEST = lax.Precision.HIGHEST


def phase_table(first, second, period):
    turned = first * second % period
    angles = turned.astype(jnp.float32) * (2.0 * math.pi / period)
    return (jnp.cos(angles), jnp.sin(angles))


def transpose_rows(values):
    return lax.all_to_all(
        values.astype(jnp.bfloat16), "seq", split_axis=1, concat_axis=0, tiled=True
    ).astype(values.dtype)


def filter_values(residues, decay_rates, positions):
    decayed = jnp.exp(-decay_rates[:, None, None, :] * positions[None, :, :, None])
    return jnp.sum(residues[:, None, None, :] * decayed, axis=0)


def forward_sum(table, values):
    return jnp.einsum("rk,risc->kisc", table, values, precision=HIGHEST)


def inverse_sum(table, values):
    return jnp.einsum("kr,kic->irc", table, values, precision=HIGHEST)


def local(tokens, in_weight, residues, decay_rates, skip_gain, out_weight):
    seq_count = lax.axis_size("seq")
    seq_index = lax.axis_index("seq")
    channels = in_weight.shape[2]
    features = in_weight.shape[0]
    all_rows = tokens.shape[0] * lax.axis_size("tp")
    block_rows = all_rows // seq_count
    stride_rows = block_rows // seq_count
    padded_size = 2 * all_rows
    gathered = lax.all_gather(tokens, "tp", axis=0, tiled=True)
    flat_weight = in_weight.reshape(features, 3 * channels)
    row_block = gathered
    projected = lax.psum_scatter(
        jnp.dot(row_block, flat_weight, preferred_element_type=jnp.float32).astype(jnp.bfloat16),
        "seq",
        scatter_dimension=0,
        tiled=True,
    )
    projected = projected.reshape(block_rows, 3, channels)
    query = projected[:, 0, :].astype(jnp.float32)
    signal = projected[:, 1, :].astype(jnp.float32) * projected[:, 2, :].astype(jnp.float32)
    lane_index = jnp.arange(stride_rows, dtype=jnp.int32)
    block_index = jnp.arange(seq_count, dtype=jnp.int32)
    local_rows = seq_index * stride_rows + lane_index
    positions = (seq_index * block_rows + jnp.arange(block_rows, dtype=jnp.int32)).astype(
        jnp.float32
    )[None, :]
    stacked = jnp.stack(
        [signal, filter_values(residues, decay_rates, positions).reshape(signal.shape)], axis=-2
    )
    signal_count = stacked.shape[-2]
    spread = transpose_rows(stacked.reshape(1, block_rows, signal_count * channels))
    spread = spread.reshape(seq_count, stride_rows, signal_count, channels)
    coarse_freq = jnp.arange(2 * seq_count, dtype=jnp.int32)
    cos_block, sin_block = phase_table(block_index[:, None], coarse_freq[None, :], 2 * seq_count)
    real_low = jnp.einsum("bk,bjsc->jksc", cos_block, spread, precision=HIGHEST)
    imag_low = -jnp.einsum("bk,bjsc->jksc", sin_block, spread, precision=HIGHEST)
    cos_twist, sin_twist = phase_table(local_rows[:, None], coarse_freq[None, :], padded_size)
    cos_twist = cos_twist[:, :, None, None]
    sin_twist = sin_twist[:, :, None, None]
    real_twist = real_low * cos_twist + imag_low * sin_twist
    imag_twist = imag_low * cos_twist - real_low * sin_twist
    packed = jnp.stack([real_twist, imag_twist], axis=2).reshape(
        stride_rows, 2 * seq_count, 2 * signal_count * channels
    )
    arrived = transpose_rows(packed).reshape(block_rows, 2, 2, signal_count, channels)
    span_index = jnp.arange(block_rows, dtype=jnp.int32)
    cos_fine, sin_fine = phase_table(span_index[:, None], span_index[None, :], block_rows)
    real_input = arrived[:, :, 0]
    imag_input = arrived[:, :, 1]
    real_high = forward_sum(cos_fine, real_input) + forward_sum(sin_fine, imag_input)
    imag_high = forward_sum(cos_fine, imag_input) - forward_sum(sin_fine, real_input)
    own_coarse = seq_index * 2 + jnp.arange(2, dtype=jnp.int32)
    filter_real = real_high[:, :, 1]
    filter_imag = imag_high[:, :, 1]
    signal_real = real_high[:, :, 0]
    signal_imag = imag_high[:, :, 0]
    product_real = signal_real * filter_real - signal_imag * filter_imag
    product_imag = signal_real * filter_imag + signal_imag * filter_real
    back_real = inverse_sum(cos_fine, product_real) - inverse_sum(sin_fine, product_imag)
    back_imag = inverse_sum(cos_fine, product_imag) + inverse_sum(sin_fine, product_real)
    cos_undo, sin_undo = phase_table(own_coarse[:, None], span_index[None, :], padded_size)
    cos_undo = cos_undo[:, :, None]
    sin_undo = sin_undo[:, :, None]
    turn_real = back_real * cos_undo - back_imag * sin_undo
    turn_imag = back_imag * cos_undo + back_real * sin_undo
    packed_back = jnp.stack([turn_real, turn_imag], axis=2).reshape(2, block_rows, 2 * channels)
    returned = transpose_rows(packed_back).reshape(2 * seq_count, stride_rows, 2, channels)
    cos_last, sin_last = phase_table(coarse_freq[:, None], block_index[None, :], 2 * seq_count)
    inverse_scale = 1.0 / padded_size
    convolved = (
        jnp.einsum("kb,kjc->jbc", cos_last, returned[:, :, 0], precision=HIGHEST)
        - jnp.einsum("kb,kjc->jbc", sin_last, returned[:, :, 1], precision=HIGHEST)
    ) * inverse_scale
    convolved = transpose_rows(convolved).reshape(block_rows, channels)
    gated = (query * (convolved + skip_gain * signal)).astype(jnp.bfloat16)
    framed = gated.reshape(1, block_rows, channels)
    whole = lax.all_gather(framed, "seq", axis=1, tiled=True).reshape(all_rows, channels)
    row_block = whole
    return lax.psum_scatter(
        jnp.dot(row_block, out_weight, preferred_element_type=jnp.float32).astype(jnp.bfloat16),
        "tp",
        scatter_dimension=0,
        tiled=True,
    )


def solution(mesh):
    in_specs = (
        P("tp", "seq"),
        P("seq", None, "tp"),
        P(None, "tp"),
        P(None, "tp"),
        P("tp"),
        P("tp", "seq"),
    )
    out_specs = P("tp", "seq")
    return jax.shard_map(local, mesh=mesh, in_specs=in_specs, out_specs=out_specs, check_vma=False)
```

profile of v0, /device:TPU:32, one launch (start us, length us, event | category | flops | bytes accessed | tf_op | source)
XLA Modules:
  0.0 447.6 jit_solution(17761818584911846178)
XLA Ops:
  7.3 4.7 %copy.91 = bf16[512,3,1024]{0,2,1:T(8,128)(2,1)} copy(bf16[512,3,1024]{2,0,1:T(8,128)(2,1)} %param.7) | data formatting | bytes 6291456 | tf_op args[1]
  12.0 49.8 %all-gather.3.cloned.1.call-done = bf16[2048,512]{1,0:T(8,128)(2,1)} async-done(((bf16[256,512]{1,0:T(8,128)(2,1)}), bf16[2048,512]{1,0:T(8,128)(2,1)}) %all-gather.3.cloned.1.call-update) | async-done | bytes 2097168 | tf_op jit(solution)/shard_map/all_gather | solution.py:45
  61.8 11.8 %convolution_convert_fusion = bf16[2048,3072]{1,0:T(8,128)(2,1)} fusion(bf16[2048,512]{1,0:T(8,128)(2,1)} %all-gather.3.cloned.1.call-done, bf16[512,3072]{0,1:T(8,128)(2,1)} %bitcast.146), kind=kOutput, calls=%fused_computation | convolution fusion | flops 6448742400 | bytes 17825792 | tf_op jit(solution)/shard_map/dot_general | solution.py:49
  74.5 1.4 multiply_reduce_fusion
  76.1 120.0 %reduce-scatter.3.cloned.1.call-done = bf16[128,3072]{1,0:T(8,128)(2,1)} async-done(((bf16[2048,3072]{1,0:T(8,128)(2,1)}), bf16[128,3072]{1,0:T(8,128)(2,1)}) %reduce-scatter.3.cloned.1.call-update) | async-done | bytes 786448 | tf_op jit(solution)/shard_map/reduce_scatter | solution.py:48
  196.1 1.5 copy.92
  199.2 3.7 reduce.3
  202.9 1.3 reshape.303
  204.2 5.2 %all-to-all-start = ((bf16[16,2,8192]{2,1,0:T(2,128)(2,1)}), bf16[16,2,8192]{2,1,0:T(2,128)(2,1)S(1)}, u32[]{:S(2)}, u32[]{:S(2)}) async-start(bf16[16,2,8192]{2,1,0:T(2,128)(2,1)} %reshape.303), calls=%async_computation.1 | async-start | bytes 1048576 | tf_op jit(solution)/shard_map/all_to_all | solution.py:18
  209.6 8.6 %all-to-all-done = bf16[16,2,8192]{2,1,0:T(2,128)(2,1)S(1)} async-done(((bf16[16,2,8192]{2,1,0:T(2,128)(2,1)}), bf16[16,2,8192]{2,1,0:T(2,128)(2,1)S(1)}, u32[]{:S(2)}, u32[]{:S(2)}) %all-to-all-start) | async-done | bytes 524320 | tf_op jit(solution)/shard_map/all_to_all | solution.py:18
  218.7 3.0 bitcast_reduce_fusion
  223.4 1.7 fusion.8
  225.3 2.2 copy.129
  227.4 2.8 reshape.301
  230.2 7.2 %all-to-all-start.1 = ((bf16[8,32,4096]{2,0,1:T(8,128)(2,1)}), bf16[8,32,4096]{2,0,1:T(8,128)(2,1)S(1)}, u32[]{:S(2)}, u32[]{:S(2)}) async-start(bf16[8,32,4096]{2,0,1:T(8,128)(2,1)} %reshape.301), calls=%async_computation.2 | async-start | bytes 4194304 | tf_op jit(solution)/shard_map/all_to_all | solution.py:18
  237.6 27.0 %all-to-all-done.1 = bf16[8,32,4096]{2,0,1:T(8,128)(2,1)S(1)} async-done(((bf16[8,32,4096]{2,0,1:T(8,128)(2,1)}), bf16[8,32,4096]{2,0,1:T(8,128)(2,1)S(1)}, u32[]{:S(2)}, u32[]{:S(2)}) %all-to-all-start.1) | async-done | bytes 2097184 | tf_op jit(solution)/shard_map/all_to_all | solution.py:18
  264.6 1.5 copy.156
  266.1 3.3 reshape.285
  269.4 1.7 fusion.137
  271.0 1.3 fusion.16
  273.6 1.3 convolution_add_fusion
  275.0 1.3 convolution_subtract_fusion
  276.9 2.0 fusion.10
  278.9 2.0 fusion.14
  280.8 2.0 convolution_add_fusion.1
  282.8 2.3 fusion.18
  286.3 22.5 %all_to_all.48 = bf16[2,128,2048]{2,0,1:T(2,128)(2,1)S(1)} all-to-all(bf16[2,128,2048]{2,0,1:T(2,128)(2,1)S(1)} %copy.111), channel_id=1, replica_groups=mesh['seq'=16,'tp'=8] {'seq'}, dimensions={1} | all-to-all | bytes 2097152 | tf_op jit(solution)/shard_map/all_to_all | solution.py:18
  310.1 2.3 fusion.138
  314.3 13.1 %all_to_all.49 = bf16[8,16,1024]{2,0,1:T(8,128)(2,1)S(1)} all-to-all(bf16[8,16,1024]{2,0,1:T(8,128)(2,1)S(1)} %copy.116), channel_id=1, replica_groups=mesh['seq'=16,'tp'=8] {'seq'}, dimensions={1} | all-to-all | bytes 524288 | tf_op jit(solution)/shard_map/all_to_all | solution.py:18
  328.6 55.2 %all-gather.5.cloned.1.call-done = bf16[1,2048,1024]{1,2,0:T(8,128)(2,1)} async-done(((bf16[1,128,1024]{1,2,0:T(8,128)(2,1)}), bf16[1,2048,1024]{1,2,0:T(8,128)(2,1)}) %all-gather.5.cloned.1.call-update) | async-done | bytes 4194320 | tf_op jit(solution)/shard_map/all_gather | solution.py:113
  383.8 5.9 %fusion.2 = bf16[2048,512]{1,0:T(8,128)(2,1)} fusion(bf16[1024,512]{1,0:T(8,128)(2,1)S(1)} %copy-done, bf16[1,2048,1024]{1,2,0:T(8,128)(2,1)} %all-gather.5.cloned.1.call-done), kind=kOutput, calls=%fused_computation.4 | convolution fusion | flops 2148532224 | bytes 7340032 | tf_op jit(solution)/shard_map/dot_general | solution.py:116
  389.7 51.1 %reduce-scatter.5.cloned.1.call-done = bf16[256,512]{1,0:T(8,128)(2,1)} async-done(((bf16[2048,512]{1,0:T(8,128)(2,1)}), bf16[256,512]{1,0:T(8,128)(2,1)}) %reduce-scatter.5.cloned.1.call-update) | async-done | bytes 262160 | tf_op jit(solution)/shard_map/reduce_scatter | solution.py:115
  (49 shorter events, 13.4 us)
Async XLA Ops:
  6.5 377.3 %copy-start = (bf16[1024,512]{1,0:T(8,128)(2,1)S(1)}, bf16[1024,512]{1,0:T(8,128)(2,1)}, u32[]{:S(2)}) copy-start(bf16[1024,512]{1,0:T(8,128)(2,1)} %param.11) | copy-start | bytes 3145732
  6.5 55.3 %all-gather.3.cloned.1.call-start = ((), (), s32[]{:S(2)}) async-start(), calls=%async_computation.6 | async-start | bytes 2359296 | tf_op jit(solution)/shard_map/all_gather | solution.py:45
  7.3 188.8 %reduce-scatter.3.cloned.1.call-start = ((), (), s32[]{:S(2)}) async-start(), calls=%async_computation.7 | async-start | bytes 13369344 | tf_op jit(solution)/shard_map/reduce_scatter | solution.py:48
  73.6 0.8 copy-start.3
  73.6 0.9 copy-start.5
  197.6 5.3 %copy-start.1 = (bf16[128,3072]{0,1:T(8,128)(2,1)}, bf16[128,3072]{0,1:T(8,128)(2,1)S(1)}, u32[]{:S(2)}) copy-start(bf16[128,3072]{0,1:T(8,128)(2,1)S(1)} %copy.92) | copy-start | bytes 2359300
  204.2 14.0 %all-to-all-start = ((bf16[16,2,8192]{2,1,0:T(2,128)(2,1)}), bf16[16,2,8192]{2,1,0:T(2,128)(2,1)S(1)}, u32[]{:S(2)}, u32[]{:S(2)}) async-start(bf16[16,2,8192]{2,1,0:T(2,128)(2,1)} %reshape.303), calls=%async_computation.1 | async-start | bytes 1048576 | tf_op jit(solution)/shard_map/all_to_all | solution.py:18
  230.2 34.3 %all-to-all-start.1 = ((bf16[8,32,4096]{2,0,1:T(8,128)(2,1)}), bf16[8,32,4096]{2,0,1:T(8,128)(2,1)S(1)}, u32[]{:S(2)}, u32[]{:S(2)}) async-start(bf16[8,32,4096]{2,0,1:T(8,128)(2,1)} %reshape.301), calls=%async_computation.2 | async-start | bytes 4194304 | tf_op jit(solution)/shard_map/all_to_all | solution.py:18
  237.4 146.4 %all-gather.5.cloned.1.call-start = ((), (), s32[]{:S(2)}) async-start(), calls=%async_computation.8 | async-start | bytes 4456448 | tf_op jit(solution)/shard_map/all_gather | solution.py:113
  313.2 14.4 %copy-start.2 = (bf16[128,3072]{0,1:T(8,128)(2,1)S(1)}, bf16[128,3072]{0,1:T(8,128)(2,1)}, u32[]{:S(2)}) copy-start(bf16[128,3072]{0,1:T(8,128)(2,1)} %copy-done.1) | copy-start | bytes 2359300
  313.2 14.4 %copy-start.4 = (f32[1024]{0:T(1024)S(1)}, f32[1024]{0:T(1024)}, u32[]{:S(2)}) copy-start(f32[1024]{0:T(1024)} %param.10) | copy-start | bytes 12292
  328.6 112.3 %reduce-scatter.5.cloned.1.call-start = ((), (), s32[]{:S(2)}) async-start(), calls=%async_computation.9 | async-start | bytes 2359296 | tf_op jit(solution)/shard_map/reduce_scatter | solution.py:115
Sparse Core Ops, SparseCore 0:
  9.0 52.7 all-gather.2
  73.7 122.2 reduce-scatter.2
  328.7 55.0 all-gather.4
  389.9 50.9 reduce-scatter.4
where the time goes:
time: 455 us; the launch traced here: 448 us
  waiting for transfers between devices  312 us (69%)
  matrix products  35.7 us (8%)
  blocking collectives  35.6 us (8%)
  local copies, waits for them, and re-layouts  30.2 us (7%)
  between operations  13.7 us (3%)
  starting transfers between devices  12.5 us (3%)
  other arithmetic  7.38 us (2%)
    reduce_scatter x1, waiting for transfers between devices, local(): lax.psum_scatter(jnp.dot(row_block, flat_weight, preferred_element_type=j...  120 us
    all_gather x1, waiting for transfers between devices, local(): lax.all_gather(framed, 'seq', axis=1, tiled=True)  55.2 us
    reduce_scatter x1, waiting for transfers between devices, local(): lax.psum_scatter(jnp.dot(row_block, out_weight, preferred_element_type=jn...  51.1 us
    all_gather x1, waiting for transfers between devices, local(): gathered = lax.all_gather(tokens, 'tp', axis=0, tiled=True)  49.8 us
    all_to_all x2, blocking collectives, transpose_rows(): lax.all_to_all(values.astype(jnp.bfloat16), 'seq', split_axis=1, concat_a...  35.6 us
    all_to_all x2, waiting for transfers between devices, transpose_rows(): lax.all_to_all(values.astype(jnp.bfloat16), 'seq', split_axis=1, concat_a...  35.6 us
    all_to_all x2, starting transfers between devices, transpose_rows(): lax.all_to_all(values.astype(jnp.bfloat16), 'seq', split_axis=1, concat_a...  12.4 us
    dot_general x1, matrix products, local(): jnp.dot(row_block, flat_weight, preferred_element_type=jnp.float32)  11.8 us
  transfers between devices with their start and end apart: 6, of which 6 were waited for; matrix products, arithmetic and copies ran while one was open for 1% of the time, Pallas kernels for 0%

commit v1 on v0

v1 whole, which is shorter than its diff:
```python
import functools

import jax
import jax.numpy as jnp
from jax import lax
from jax.experimental import pallas as pl
from jax.experimental.pallas import tpu as pltpu
from jax.sharding import PartitionSpec as P

MESH = pl.DeviceIdType.MESH
F32 = jnp.float32
BF16 = jnp.bfloat16
CHUNKS = 8
ROWS = 128
HALF = 64
LANES = 128
MODES = 16
SEGS = 8
STEPS = 16
QKV = 3 * LANES
FEATURES = 512
WIDE = 1024


def remote(src, dst, send_sem, recv_sem, device):
    return pltpu.make_async_remote_copy(
        src_ref=src,
        dst_ref=dst,
        send_sem=send_sem,
        recv_sem=recv_sem,
        device_id=device,
        device_id_type=MESH,
    )


def wait_bytes(ref, sem):
    pltpu.make_async_copy(ref, ref, sem).wait()


def aligned(value, step):
    return pl.multiple_of(value * step, step)


def kernel(
    tokens,
    in_weight,
    residues,
    decay_rates,
    skip_gain,
    out_weight,
    out,
    tok,
    w_in,
    w_out,
    part,
    relay,
    direct,
    summed,
    y_send,
    y_recv,
    s_scr,
    y_scr,
    q_scr,
    decay_b,
    res_b,
    seg_b,
    scan_b,
    ends,
    state_in,
    state_out,
    gath,
    p_out,
    o_relay,
    o_dir,
    o_sum,
    o_acc,
    o_y,
    o_fin,
    local_sem,
    tok_sem,
    w_sem,
    wo_sem,
    relay_sem,
    direct_sem,
    summed_sem,
    y_sem,
    state_sem,
    gath_sem,
    o_relay_sem,
    o_dir_sem,
    o_sum_sem,
    o_y_sem,
    fin_sem,
    send_sem,
):
    seq = lax.axis_index("seq")
    tp = lax.axis_index("tp")
    core = lax.rem(seq, 2)
    z = lax.rem(seq // 2, 4)
    y_hi = seq // 8
    x = tp // 2
    y_lo = lax.rem(tp, 2)

    def at(dx=0, dz=0, flip_hi=False, flip_lo=False, flip_core=False):
        a = 1 - y_hi if flip_hi else y_hi
        b = lax.rem(z + dz, 4)
        c = 1 - core if flip_core else core
        d = lax.rem(x + dx, 4)
        e = 1 - y_lo if flip_lo else y_lo
        return (a * 8 + b * 2 + c, d * 2 + e)

    sibling = at(flip_core=True)
    z_next, z_prev, z_far = at(dz=1), at(dz=3), at(dz=2)
    y_far = at(flip_hi=True)
    x_next, x_prev, x_far = at(dx=1), at(dx=3), at(dx=2)
    y_near = at(flip_lo=True)
    peers = [sibling, z_next, z_prev, z_far, y_far, x_next, x_prev, x_far, y_near]
    block = y_hi * 4 + z
    lanes = pl.ds(aligned(block, LANES), LANES)

    barrier = pltpu.get_barrier_semaphore()
    for peer in peers:
        pl.semaphore_signal(barrier, inc=1, device_id=peer, device_id_type=MESH)
    pl.semaphore_wait(barrier, len(peers))

    own_rows = pl.ds(aligned(core, ROWS), ROWS)
    other_rows = pl.ds(aligned(1 - core, ROWS), ROWS)
    own_feat = pl.ds(aligned(core, FEATURES), FEATURES)
    other_feat = pl.ds(aligned(1 - core, FEATURES), FEATURES)
    tok_local = pltpu.make_async_copy(tokens.at[own_rows, :], tok.at[tp, :, own_feat], local_sem.at[0])
    tok_local.start()
    remote(tokens.at[other_rows, :], tok.at[tp, :, own_feat], send_sem.at[0], tok_sem.at[CHUNKS], sibling).start()

    def weight_pair(r):
        zi = lax.rem(z + r, 4)
        return in_weight.at[zi], w_in.at[zi, own_feat, :], w_in.at[zi, other_feat, :]

    for r in (2, 1, 3, 0):
        src, dst, _ = weight_pair(r)
        pltpu.make_async_copy(src, dst, local_sem.at[1 + r]).start()
        remote(src, dst, send_sem.at[1], w_sem.at[r], sibling).start()
    pltpu.make_async_copy(out_weight, w_out.at[core], local_sem.at[5]).start()

    seg_index = lax.broadcasted_iota(jnp.int32, (SEGS, LANES), 0)
    seg_next = (seg_index + 1).astype(F32) * float(STEPS)
    for m in range(MODES):
        rate = jnp.broadcast_to(decay_rates[pl.ds(m, 1), lanes], (SEGS, LANES))
        decay_b[m] = jnp.exp(-rate)
        res_b[m] = jnp.broadcast_to(residues[pl.ds(m, 1), lanes], (SEGS, LANES))
        seg_b[m] = jnp.exp(-rate * seg_next)
        for k in range(3):
            scan_b[k, m] = jnp.where(seg_index >= (1 << k), jnp.exp(-rate * float(STEPS << k)), 0.0)

    @pl.when(core == 0)
    def _():
        state_in[0] = jnp.zeros((MODES, LANES), F32)

    tok_local.wait()
    wait_bytes(tok.at[0, :, pl.ds(0, FEATURES)], tok_sem.at[CHUNKS])
    for peer in (y_near, x_next, x_prev, x_far):
        remote(tok.at[tp], tok.at[tp], send_sem.at[0], tok_sem.at[tp], peer).start()
    remote(out_weight, w_out.at[core], send_sem.at[1], wo_sem.at[0], sibling).start()

    near = x * 2 + 1 - y_lo

    def order(i):
        return jnp.where(i == 0, tp, jnp.where(i <= tp, i - 1, i))

    def multiply(jc, r):
        zi = lax.rem(z + r, 4)

        def column(n, carry):
            cols = pl.ds(aligned(n, 256), 256)
            acc = jnp.dot(tok[jc], w_in[zi, :, cols], preferred_element_type=F32)
            part[jc, r, :, cols] = acc.astype(BF16)
            return carry

        lax.fori_loop(0, 3, column, 0)

    first, second = pl.ds(0, QKV), pl.ds(QKV, QKV)

    def project(i):
        jc = order(i)

        @pl.when(jnp.logical_and(i > 0, jc != near))
        def _():
            wait_bytes(tok.at[jc], tok_sem.at[jc])

        for r in (2, 1, 3, 0):

            @pl.when(i == 0)
            def _():
                src, dst, other = weight_pair(r)
                pltpu.make_async_copy(src, dst, local_sem.at[1 + r]).wait()
                wait_bytes(other, w_sem.at[r])

            multiply(jc, r)
            if r == 2:
                remote(part.at[jc, 2, :, first], relay.at[0, jc], send_sem.at[2], relay_sem.at[0, jc], z_next).start()
                remote(part.at[jc, 2, :, second], relay.at[1, jc], send_sem.at[2], relay_sem.at[1, jc], z_prev).start()
            elif r == 1:
                remote(part.at[jc, 1, :, second], direct.at[1, jc], send_sem.at[3], direct_sem.at[1, jc], z_next).start()
            elif r == 3:
                remote(part.at[jc, 3, :, first], direct.at[0, jc], send_sem.at[3], direct_sem.at[0, jc], z_prev).start()

    def pass_on(jc):
        for k, r, cols, peer in ((0, 1, first, z_next), (1, 3, second, z_prev)):
            wait_bytes(relay.at[k, jc], relay_sem.at[k, jc])
            relay[k, jc] = (relay[k, jc].astype(F32) + part[jc, r, :, cols].astype(F32)).astype(BF16)
            remote(relay.at[k, jc], summed.at[k, jc], send_sem.at[4], summed_sem.at[k, jc], peer).start()

    def gather_half(jc, k):
        cols = pl.ds(aligned(k, QKV), QKV)
        return part[jc, 0, :, cols].astype(F32) + direct[k, jc].astype(F32) + summed[k, jc].astype(F32)

    def cross(jc):
        for k in range(2):
            wait_bytes(direct.at[k, jc], direct_sem.at[k, jc])
            wait_bytes(summed.at[k, jc], summed_sem.at[k, jc])
        y_send[jc] = gather_half(jc, 1 - y_hi).astype(BF16)
        remote(y_send.at[jc], y_recv.at[jc], send_sem.at[5], y_sem.at[jc], y_far).start()

    def convolve(j):
        wait_bytes(y_recv.at[j], y_sem.at[j])
        total = gather_half(j, y_hi) + y_recv[j].astype(F32)
        q_scr[...] = total[:, :LANES]
        s_scr[...] = total[:, LANES : 2 * LANES] * total[:, 2 * LANES :]
        decay = [decay_b[m] for m in range(MODES)]
        held = [jnp.zeros((SEGS, LANES), F32)] * MODES
        for i in range(STEPS):
            now = s_scr[pl.ds(i, SEGS, stride=STEPS), :]
            held = [decay[m] * held[m] + now for m in range(MODES)]
        for m in range(MODES):
            total = held[m]
            for k in range(3):
                total = total + scan_b[k, m] * pltpu.roll(total, 1 << k, 0)
            ends[m] = total

        @pl.when(jnp.logical_or(core == 1, j > 0))
        def _():
            wait_bytes(state_in.at[j], state_sem.at[j])

        for m in range(MODES):
            before = jnp.broadcast_to(state_in[j, pl.ds(m, 1), :], (SEGS, LANES))
            full = ends[m] + seg_b[m] * before
            state_out[j, pl.ds(m, 1), :] = full[SEGS - 1 :, :]
            ends[m] = jnp.where(seg_index == 0, before, pltpu.roll(full, 1, 0))

        @pl.when(jnp.logical_or(core == 0, j < CHUNKS - 1))
        def _():
            remote(state_out.at[j], state_in.at[j + core], send_sem.at[6], state_sem.at[j + core], sibling).start()

        held = [ends[m] for m in range(MODES)]
        for i in range(STEPS):
            now = s_scr[pl.ds(i, SEGS, stride=STEPS), :]
            held = [decay_b[m] * held[m] + now for m in range(MODES)]
            terms = [res_b[m] * held[m] for m in range(MODES)]
            while len(terms) > 1:
                terms = [terms[k] + terms[k + 1] for k in range(0, len(terms), 2)]
            y_scr[pl.ds(i, SEGS, stride=STEPS), :] = terms[0]
        gain = skip_gain[:, lanes]
        gath[j, :, lanes] = (q_scr[...] * (y_scr[...] + gain * s_scr[...])).astype(BF16)
        own = gath.at[j, :, lanes]
        for peer in (z_next, z_prev, z_far, y_far):
            remote(own, own, send_sem.at[7], gath_sem.at[block, j], peer).start()

    def forward(j):
        for r in (1, 3, 2):
            b = y_hi * 4 + lax.rem(z + r, 4)
            there = gath.at[j, :, pl.ds(aligned(b, LANES), LANES)]
            wait_bytes(there, gath_sem.at[b, j])
            remote(there, there, send_sem.at[7], gath_sem.at[b, j], y_far).start()

    upper, lower = pl.ds(0, HALF), pl.ds(HALF, HALF)

    def distance(j):
        return lax.rem(j // 2 - x + 4, 4)

    def finish(j):
        for r in range(4):
            b = (1 - y_hi) * 4 + r
            wait_bytes(gath.at[j, :, pl.ds(aligned(b, LANES), LANES)], gath_sem.at[b, j])

        @pl.when(j == 0)
        def _():
            pltpu.make_async_copy(out_weight, w_out.at[core], local_sem.at[5]).wait()
            wait_bytes(w_out.at[1 - core], wo_sem.at[0])

        for h in range(2):

            def column(n, carry):
                cols = pl.ds(aligned(n, 256), 256)
                acc = jnp.dot(gath[j], w_out[h, :, cols], preferred_element_type=F32)
                p_out[j, :, pl.ds(pl.multiple_of(h * FEATURES + n * 256, 256), 256)] = acc.astype(BF16)
                return carry

            lax.fori_loop(0, 2, column, 0)
        dx = distance(j)
        side = lax.rem(j, 2)

        @pl.when(dx == 2)
        def _():
            remote(p_out.at[j, upper], o_relay.at[j], send_sem.at[8], o_relay_sem.at[j], x_next).start()
            remote(p_out.at[j, lower], o_relay.at[j], send_sem.at[8], o_relay_sem.at[j], x_prev).start()

        @pl.when(dx == 1)
        def _():
            remote(p_out.at[j, lower], o_dir.at[1, side], send_sem.at[8], o_dir_sem.at[1, side], x_next).start()

        @pl.when(dx == 3)
        def _():
            remote(p_out.at[j, upper], o_dir.at[0, side], send_sem.at[8], o_dir_sem.at[0, side], x_prev).start()

    def o_pass(j):
        dx = distance(j)
        side = lax.rem(j, 2)
        for want, rows, k, peer in ((1, upper, 0, x_next), (3, lower, 1, x_prev)):

            @pl.when(dx == want)
            def _():
                wait_bytes(o_relay.at[j], o_relay_sem.at[j])
                o_relay[j] = (o_relay[j].astype(F32) + p_out[j, rows, :].astype(F32)).astype(BF16)
                remote(o_relay.at[j], o_sum.at[k, side], send_sem.at[8], o_sum_sem.at[k, side], peer).start()

    def o_cross(j):
        side = lax.rem(j, 2)

        @pl.when(distance(j) == 0)
        def _():
            for k in range(2):
                wait_bytes(o_dir.at[k, side], o_dir_sem.at[k, side])
                wait_bytes(o_sum.at[k, side], o_sum_sem.at[k, side])

            def total(k, rows):
                return p_out[j, rows, :].astype(F32) + o_dir[k, side].astype(F32) + o_sum[k, side].astype(F32)

            @pl.when(side == y_lo)
            def _():
                for k, rows in ((0, upper), (1, lower)):
                    o_acc[rows, :] = total(k, rows)

            @pl.when(side != y_lo)
            def _():
                for k, rows in ((0, upper), (1, lower)):
                    p_out[j, rows, :] = total(k, rows).astype(BF16)
                remote(p_out.at[j], o_y, send_sem.at[8], o_y_sem.at[0], y_near).start()

    def o_last(j):
        @pl.when(j == tp)
        def _():
            wait_bytes(o_y, o_y_sem.at[0])
            mine = pl.ds(aligned(core, FEATURES), FEATURES)
            theirs = pl.ds(aligned(1 - core, FEATURES), FEATURES)
            o_fin[...] = (o_acc[:, theirs] + o_y[:, theirs].astype(F32)).astype(BF16)
            remote(o_fin, out.at[own_rows, :], send_sem.at[8], fin_sem.at[0], sibling).start()
            out[own_rows, :] = (o_acc[:, mine] + o_y[:, mine].astype(F32)).astype(BF16)

    def step(i, carry):
        def stage(lag, body):
            @pl.when(jnp.logical_and(i >= lag, i < lag + CHUNKS))
            def _():
                body(i - lag)

        @pl.when(i == 1)
        def _():
            wait_bytes(tok.at[near], tok_sem.at[near])
            for peer in (x_next, x_prev, x_far):
                remote(tok.at[near], tok.at[near], send_sem.at[0], tok_sem.at[near], peer).start()

        stage(0, project)
        stage(1, lambda k: pass_on(order(k)))
        stage(2, lambda k: cross(order(k)))
        stage(4, convolve)
        stage(5, forward)
        stage(6, finish)
        stage(7, o_pass)
        stage(8, o_cross)
        stage(9, o_last)
        return carry

    lax.fori_loop(0, CHUNKS + 9, step, 0)

    wait_bytes(o_fin, fin_sem.at[0])
    wait_bytes(tok.at[pl.ds(0, 7)], send_sem.at[0])
    wait_bytes(tok.at[0, :, pl.ds(0, FEATURES)], send_sem.at[0])
    wait_bytes(in_weight, send_sem.at[1])
    wait_bytes(out_weight, send_sem.at[1])
    wait_bytes(relay, send_sem.at[2])
    wait_bytes(direct, send_sem.at[3])
    wait_bytes(summed, send_sem.at[4])
    wait_bytes(y_recv, send_sem.at[5])
    wait_bytes(state_out.at[pl.ds(0, CHUNKS - 1)], send_sem.at[6])

    @pl.when(core == 0)
    def _():
        wait_bytes(state_out.at[0], send_sem.at[6])

    wait_bytes(gath.at[pl.ds(0, 7)], send_sem.at[7])
    wait_bytes(p_out.at[pl.ds(0, 7)], send_sem.at[8])
    wait_bytes(o_fin, send_sem.at[8])


def local(tokens, in_weight, residues, decay_rates, skip_gain, out_weight):
    features, _, channels = in_weight.shape
    sorted_weight = in_weight.reshape(features, 3, 2, 4, LANES).transpose(3, 0, 2, 1, 4).reshape(4, features, 2 * QKV)
    vmem = pl.BlockSpec(memory_space=pltpu.VMEM)
    anywhere = pl.BlockSpec(memory_space=pl.ANY)
    dma = pltpu.SemaphoreType.DMA
    scratch = [
        pltpu.VMEM((CHUNKS, ROWS, WIDE), BF16),
        pltpu.VMEM((4, WIDE, 2 * QKV), BF16),
        pltpu.VMEM((2, WIDE, FEATURES), BF16),
        pltpu.VMEM((CHUNKS, 4, ROWS, 2 * QKV), BF16),
        pltpu.VMEM((2, CHUNKS, ROWS, QKV), BF16),
        pltpu.VMEM((2, CHUNKS, ROWS, QKV), BF16),
        pltpu.VMEM((2, CHUNKS, ROWS, QKV), BF16),
        pltpu.VMEM((CHUNKS, ROWS, QKV), BF16),
        pltpu.VMEM((CHUNKS, ROWS, QKV), BF16),
        pltpu.VMEM((ROWS, LANES), F32),
        pltpu.VMEM((ROWS, LANES), F32),
        pltpu.VMEM((ROWS, LANES), F32),
        pltpu.VMEM((MODES, SEGS, LANES), F32),
        pltpu.VMEM((MODES, SEGS, LANES), F32),
        pltpu.VMEM((MODES, SEGS, LANES), F32),
        pltpu.VMEM((3, MODES, SEGS, LANES), F32),
        pltpu.VMEM((MODES, SEGS, LANES), F32),
        pltpu.VMEM((CHUNKS + 1, MODES, LANES), F32),
        pltpu.VMEM((CHUNKS, MODES, LANES), F32),
        pltpu.VMEM((CHUNKS, ROWS, WIDE), BF16),
        pltpu.VMEM((CHUNKS, ROWS, WIDE), BF16),
        pltpu.VMEM((CHUNKS, HALF, WIDE), BF16),
        pltpu.VMEM((2, 2, HALF, WIDE), BF16),
        pltpu.VMEM((2, 2, HALF, WIDE), BF16),
        pltpu.VMEM((ROWS, WIDE), F32),
        pltpu.VMEM((ROWS, WIDE), BF16),
        pltpu.VMEM((ROWS, FEATURES), BF16),
        dma((6,)),
        dma((CHUNKS + 1,)),
        dma((4,)),
        dma((1,)),
        dma((2, CHUNKS)),
        dma((2, CHUNKS)),
        dma((2, CHUNKS)),
        dma((CHUNKS,)),
        dma((CHUNKS + 1,)),
        dma((8, CHUNKS)),
        dma((CHUNKS,)),
        dma((2, 2)),
        dma((2, 2)),
        dma((1,)),
        dma((1,)),
        dma((9,)),
    ]
    return pl.pallas_call(
        kernel,
        out_shape=jax.ShapeDtypeStruct(tokens.shape, BF16),
        in_specs=[anywhere, anywhere, vmem, vmem, vmem, anywhere],
        out_specs=vmem,
        scratch_shapes=scratch,
        compiler_params=pltpu.CompilerParams(
            collective_id=0, has_side_effects=True, vmem_limit_bytes=56 * 2**20
        ),
        name="hyena_block",
    )(tokens, sorted_weight, residues, decay_rates, skip_gain.reshape(1, channels), out_weight)


def solution(mesh):
    in_specs = (
        P("tp", "seq"),
        P("seq", None, "tp"),
        P(None, "tp"),
        P(None, "tp"),
        P("tp"),
        P("tp", "seq"),
    )
    return jax.shard_map(local, mesh=mesh, in_specs=in_specs, out_specs=P("tp", "seq"), check_vma=False)
```

time: 455 us -> 144 us (0.32)
  the two profiles are of different devices: /device:TPU:32 before, /device:TPU:15 now
where the time goes in v1:
time: 144 us
  Pallas kernels  133 us (92%)
  local copies, waits for them, and re-layouts  11.3 us (8%)
    pallas_call x1, Pallas kernels, local(): pl.pallas_call(kernel, out_shape=jax.ShapeDtypeStruct(tokens.shape, BF16)...  133 us
    unnamed x2, local copies, waits for them, and re-layouts  6.35 us

profile of v1, /device:TPU:15, one launch (start us, length us, event | category | flops | bytes accessed | tf_op | source)
XLA Modules:
  0.0 143.9 jit_solution(2176106208180193858)
XLA Ops:
  0.0 4.7 %copy.9 = bf16[512,3,1024]{0,2,1:T(8,128)(2,1)} copy(bf16[512,3,1024]{2,0,1:T(8,128)(2,1)} %param.7) | data formatting | bytes 6291456 | tf_op args[1]
  4.7 2.2 %copy.10 = bf16[4,512,2,3,128]{1,4,3,2,0:T(8,128)(2,1)S(1)} copy(bf16[4,512,2,3,128]{1,4,0,2,3:T(8,128)(2,1)} %bitcast.6) | data formatting | bytes 6291456 | tf_op jit(solution)/shard_map/transpose | solution.py:405
  6.8 2.8 %copy.11.in_weight = bf16[4,512,768]{2,1,0:T(8,128)(2,1)} copy(bf16[4,512,768]{1,2,0:T(8,128)(2,1)S(1)} %bitcast.5) | data formatting | bytes 6291456 | tf_op jit(solution)/shard_map/reshape | solution.py:405
  9.7 132.6 %hyena_block.1 = bf16[256,512]{1,0:T(8,128)(2,1)} custom-call(bf16[256,512]{1,0:T(8,128)(2,1)} %tokens.1, bf16[4,512,768]{2,1,0:T(8,128)(2,1)} %copy.11.in_weight, f32[16,1024]{1,0:T(8,128)} %residues.1, f32[16,1024]{1,0:T(8,128)} %decay_rates.1, f32[1,1024]{1,0:T(1,128)} %bitcast.7, bf16[1024,512]{1,0:T(8,128)(2,1)} %out_weight.1), custom_call_target="tpu_custom_call" | custom-call | tf_op jit(solution)/shard_map/hyena_block/pallas_call | solution.py:454
  142.3 1.7 %copy.13 = bf16[256,512]{1,0:T(8,128)(2,1)} copy(bf16[256,512]{1,0:T(8,128)(2,1)} %hyena_block.1) | data formatting | bytes 524288

commit v2 on v1

--- a/solution.py
+++ b/solution.py
@@ -131,14 +131,19 @@
     tok_local.start()
     remote(tokens.at[other_rows, :], tok.at[tp, :, own_feat], send_sem.at[0], tok_sem.at[CHUNKS], sibling).start()
 
-    def weight_pair(r):
+    def own_weight(r):
+        return w_in.at[lax.rem(z + r, 4), own_feat, :]
+
+    for r in (2, 1, 3, 0):
         zi = lax.rem(z + r, 4)
-        return in_weight.at[zi], w_in.at[zi, own_feat, :], w_in.at[zi, other_feat, :]
-
-    for r in (2, 1, 3, 0):
-        src, dst, _ = weight_pair(r)
-        pltpu.make_async_copy(src, dst, local_sem.at[1 + r]).start()
-        remote(src, dst, send_sem.at[1], w_sem.at[r], sibling).start()
+        for h in range(2):
+            there = pl.ds(aligned(h * 4 + zi, LANES), LANES)
+            for k in range(3):
+                pltpu.make_async_copy(
+                    in_weight.at[k, :, there],
+                    w_in.at[zi, own_feat, pl.ds((h * 3 + k) * LANES, LANES)],
+                    local_sem.at[1 + r],
+                ).start()
     pltpu.make_async_copy(out_weight, w_out.at[core], local_sem.at[5]).start()
 
     seg_index = lax.broadcasted_iota(jnp.int32, (SEGS, LANES), 0)
@@ -155,6 +160,9 @@
     def _():
         state_in[0] = jnp.zeros((MODES, LANES), F32)
 
+    for r in (2, 1, 3, 0):
+        wait_bytes(own_weight(r), local_sem.at[1 + r])
+        remote(own_weight(r), own_weight(r), send_sem.at[1], w_sem.at[r], sibling).start()
     tok_local.wait()
     wait_bytes(tok.at[0, :, pl.ds(0, FEATURES)], tok_sem.at[CHUNKS])
     for peer in (y_near, x_next, x_prev, x_far):
@@ -169,13 +177,7 @@
     def multiply(jc, r):
         zi = lax.rem(z + r, 4)
 
-        def column(n, carry):
-            cols = pl.ds(aligned(n, 256), 256)
-            acc = jnp.dot(tok[jc], w_in[zi, :, cols], preferred_element_type=F32)
-            part[jc, r, :, cols] = acc.astype(BF16)
-            return carry
-
-        lax.fori_loop(0, 3, column, 0)
+        part[jc, r] = jnp.dot(tok[jc], w_in[zi], preferred_element_type=F32).astype(BF16)
 
     first, second = pl.ds(0, QKV), pl.ds(QKV, QKV)
 
@@ -190,9 +192,7 @@
 
             @pl.when(i == 0)
             def _():
-                src, dst, other = weight_pair(r)
-                pltpu.make_async_copy(src, dst, local_sem.at[1 + r]).wait()
-                wait_bytes(other, w_sem.at[r])
+                wait_bytes(w_in.at[0, other_feat, :], w_sem.at[r])
 
             multiply(jc, r)
             if r == 2:
@@ -287,14 +287,8 @@
             wait_bytes(w_out.at[1 - core], wo_sem.at[0])
 
         for h in range(2):
-
-            def column(n, carry):
-                cols = pl.ds(aligned(n, 256), 256)
-                acc = jnp.dot(gath[j], w_out[h, :, cols], preferred_element_type=F32)
-                p_out[j, :, pl.ds(pl.multiple_of(h * FEATURES + n * 256, 256), 256)] = acc.astype(BF16)
-                return carry
-
-            lax.fori_loop(0, 2, column, 0)
+            cols = pl.ds(h * FEATURES, FEATURES)
+            p_out[j, :, cols] = jnp.dot(gath[j], w_out[h], preferred_element_type=F32).astype(BF16)
         dx = distance(j)
         side = lax.rem(j, 2)
 
@@ -383,7 +377,7 @@
     wait_bytes(o_fin, fin_sem.at[0])
     wait_bytes(tok.at[pl.ds(0, 7)], send_sem.at[0])
     wait_bytes(tok.at[0, :, pl.ds(0, FEATURES)], send_sem.at[0])
-    wait_bytes(in_weight, send_sem.at[1])
+    wait_bytes(w_in.at[:, own_feat, :], send_sem.at[1])
     wait_bytes(out_weight, send_sem.at[1])
     wait_bytes(relay, send_sem.at[2])
     wait_bytes(direct, send_sem.at[3])
@@ -401,8 +395,7 @@
 
 
 def local(tokens, in_weight, residues, decay_rates, skip_gain, out_weight):
-    features, _, channels = in_weight.shape
-    sorted_weight = in_weight.reshape(features, 3, 2, 4, LANES).transpose(3, 0, 2, 1, 4).reshape(4, features, 2 * QKV)
+    channels = in_weight.shape[2]
     vmem = pl.BlockSpec(memory_space=pltpu.VMEM)
     anywhere = pl.BlockSpec(memory_space=pl.ANY)
     dma = pltpu.SemaphoreType.DMA
@@ -461,7 +454,7 @@
             collective_id=0, has_side_effects=True, vmem_limit_bytes=56 * 2**20
         ),
         name="hyena_block",
-    )(tokens, sorted_weight, residues, decay_rates, skip_gain.reshape(1, channels), out_weight)
+    )(tokens, in_weight.transpose(1, 0, 2), residues, decay_rates, skip_gain.reshape(1, channels), out_weight)
 
 
 def solution(mesh):

time: 144 us -> 133 us (0.924)
  local copies, waits for them, and re-layouts: 11.3 us -> 1.67 us
  Pallas kernels: 133 us -> 131 us
    unnamed x2 -> x1, local copies, waits for them, and re-layouts: 6.35 us -> 1.67 us
    reshape x1 -> x0, local copies, waits for them, and re-layouts: 2.81 us -> none  [local(): in_weight.reshape(features, 3, 2, 4, LANES).transpose(3, 0, 2, 1, 4)]
    transpose x1 -> x0, local copies, waits for them, and re-layouts: 2.16 us -> none  [local(): in_weight.reshape(features, 3, 2, 4, LANES).transpose(3, 0, 2, 1, 4)]
where the time goes in v2:
time: 133 us
  Pallas kernels  131 us (98%)
  local copies, waits for them, and re-layouts  1.67 us (1%)
    pallas_call x1, Pallas kernels, local(): pl.pallas_call(kernel, out_shape=jax.ShapeDtypeStruct(tokens.shape, BF16)...  131 us

profile of v2, /device:TPU:15, one launch (start us, length us, event | category | flops | bytes accessed | tf_op | source)
XLA Modules:
  0.0 133.0 jit_solution(15978271018148008427)
XLA Ops:
  0.0 131.4 %hyena_block.1 = bf16[256,512]{1,0:T(8,128)(2,1)} custom-call(bf16[256,512]{1,0:T(8,128)(2,1)} %tokens.1, bf16[3,512,1024]{2,1,0:T(8,128)(2,1)} %bitcast.2, f32[16,1024]{1,0:T(8,128)} %residues.1, f32[16,1024]{1,0:T(8,128)} %decay_rates.1, f32[1,1024]{1,0:T(1,128)} %bitcast.3, bf16[1024,512]{1,0:T(8,128)(2,1)} %out_weight.1), custom_call_target="tpu_custom_call" | custom-call | tf_op jit(solution)/shard_map/hyena_block/pallas_call | solution.py:447
  131.4 1.7 %copy.8 = bf16[256,512]{1,0:T(8,128)(2,1)} copy(bf16[256,512]{1,0:T(8,128)(2,1)} %hyena_block.1) | data formatting | bytes 524288

commit v3 on v2

--- a/solution.py
+++ b/solution.py
@@ -20,6 +20,20 @@
 QKV = 3 * LANES
 FEATURES = 512
 WIDE = 1024
+DIRECT = 6
+CONVOLVE_AT = (12, 12, 13, 14, 15, 16, 18, 19)
+FINISH_AT = (14, 14, 15, 16, 17, 18, 19, 20)
+CHUNK_ORDERS = (
+    (0, 1, 2, 3, 4, 5, 6, 7),
+    (1, 0, 3, 2, 4, 5, 6, 7),
+    (2, 3, 0, 1, 4, 5, 6, 7),
+    (3, 2, 1, 0, 4, 5, 6, 7),
+    (4, 5, 0, 2, 1, 3, 6, 7),
+    (5, 4, 1, 2, 0, 3, 6, 7),
+    (6, 0, 2, 1, 3, 4, 5, 7),
+    (7, 1, 3, 0, 2, 4, 5, 6),
+)
+ORDERS = tuple(sum(chunk << (3 * k) for k, chunk in enumerate(row)) for row in CHUNK_ORDERS)
 
 
 def remote(src, dst, send_sem, recv_sem, device):
@@ -78,6 +92,7 @@
     o_fin,
     local_sem,
     tok_sem,
+    far_sem,
     w_sem,
     wo_sem,
     relay_sem,
@@ -112,24 +127,22 @@
     sibling = at(flip_core=True)
     z_next, z_prev, z_far = at(dz=1), at(dz=3), at(dz=2)
     y_far = at(flip_hi=True)
-    x_next, x_prev, x_far = at(dx=1), at(dx=3), at(dx=2)
+    x_next, x_prev = at(dx=1), at(dx=3)
     y_near = at(flip_lo=True)
-    peers = [sibling, z_next, z_prev, z_far, y_far, x_next, x_prev, x_far, y_near]
+    diagonals = [at(dz=r, flip_hi=True) for r in (2, 1, 3)]
+    peers = [sibling, z_next, z_prev, z_far, y_far, x_next, x_prev, y_near, *diagonals]
     block = y_hi * 4 + z
     lanes = pl.ds(aligned(block, LANES), LANES)
 
     barrier = pltpu.get_barrier_semaphore()
     for peer in peers:
         pl.semaphore_signal(barrier, inc=1, device_id=peer, device_id_type=MESH)
-    pl.semaphore_wait(barrier, len(peers))
 
     own_rows = pl.ds(aligned(core, ROWS), ROWS)
     other_rows = pl.ds(aligned(1 - core, ROWS), ROWS)
     own_feat = pl.ds(aligned(core, FEATURES), FEATURES)
     other_feat = pl.ds(aligned(1 - core, FEATURES), FEATURES)
-    tok_local = pltpu.make_async_copy(tokens.at[own_rows, :], tok.at[tp, :, own_feat], local_sem.at[0])
-    tok_local.start()
-    remote(tokens.at[other_rows, :], tok.at[tp, :, own_feat], send_sem.at[0], tok_sem.at[CHUNKS], sibling).start()
+    pltpu.make_async_copy(tokens.at[own_rows, :], tok.at[tp, :, own_feat], local_sem.at[0]).start()
 
     def own_weight(r):
         return w_in.at[lax.rem(z + r, 4), own_feat, :]
@@ -146,6 +159,19 @@
                 ).start()
     pltpu.make_async_copy(out_weight, w_out.at[core], local_sem.at[5]).start()
 
+    pl.semaphore_wait(barrier, len(peers))
+    remote(tokens.at[other_rows, :], tok.at[tp, :, own_feat], send_sem.at[0], tok_sem.at[CHUNKS], sibling).start()
+    wait_bytes(own_weight(2), local_sem.at[3])
+    remote(own_weight(2), own_weight(2), send_sem.at[1], w_sem.at[2], sibling).start()
+    wait_bytes(tok.at[0, :, pl.ds(0, FEATURES)], local_sem.at[0])
+    wait_bytes(tok.at[0, :, pl.ds(0, FEATURES)], tok_sem.at[CHUNKS])
+    for peer in (y_near, x_next, x_prev):
+        remote(tok.at[tp], tok.at[tp], send_sem.at[0], tok_sem.at[tp], peer).start()
+    for r in (1, 3, 0):
+        wait_bytes(own_weight(r), local_sem.at[1 + r])
+        remote(own_weight(r), own_weight(r), send_sem.at[1], w_sem.at[r], sibling).start()
+    remote(out_weight, w_out.at[core], send_sem.at[1], wo_sem.at[0], sibling).start()
+
     seg_index = lax.broadcasted_iota(jnp.int32, (SEGS, LANES), 0)
     seg_next = (seg_index + 1).astype(F32) * float(STEPS)
     for m in range(MODES):
@@ -160,19 +186,26 @@
     def _():
         state_in[0] = jnp.zeros((MODES, LANES), F32)
 
-    for r in (2, 1, 3, 0):
-        wait_bytes(own_weight(r), local_sem.at[1 + r])
-        remote(own_weight(r), own_weight(r), send_sem.at[1], w_sem.at[r], sibling).start()
-    tok_local.wait()
-    wait_bytes(tok.at[0, :, pl.ds(0, FEATURES)], tok_sem.at[CHUNKS])
-    for peer in (y_near, x_next, x_prev, x_far):
-        remote(tok.at[tp], tok.at[tp], send_sem.at[0], tok_sem.at[tp], peer).start()
-    remote(out_weight, w_out.at[core], send_sem.at[1], wo_sem.at[0], sibling).start()
-
+    upper, lower = pl.ds(0, HALF), pl.ds(HALF, HALF)
     near = x * 2 + 1 - y_lo
+    code = jnp.int32(ORDERS[0])
+    for t in range(1, 8):
+        code = jnp.where(tp == t, jnp.int32(ORDERS[t]), code)
 
     def order(i):
-        return jnp.where(i == 0, tp, jnp.where(i <= tp, i - 1, i))
+        return lax.shift_right_logical(code, 3 * i) & 7
+
+    def column_chunk(dx, row):
+        return lax.rem(x + dx, 4) * 2 + row
+
+    def relay_tokens(row, far):
+        after, before = column_chunk(1, row), column_chunk(3, row)
+        for chunk in (after, before):
+            wait_bytes(tok.at[chunk], tok_sem.at[chunk])
+        remote(
+            tok.at[before, upper], tok.at[before, upper], send_sem.at[0], far_sem.at[far, 0], x_next
+        ).start()
+        remote(tok.at[after, lower], tok.at[after, lower], send_sem.at[0], far_sem.at[far, 1], x_prev).start()
 
     def multiply(jc, r):
         zi = lax.rem(z + r, 4)
@@ -184,9 +217,12 @@
     def project(i):
         jc = order(i)
 
-        @pl.when(jnp.logical_and(i > 0, jc != near))
-        def _():
-            wait_bytes(tok.at[jc], tok_sem.at[jc])
+        for far, row in ((0, y_lo), (1, 1 - y_lo)):
+
+            @pl.when(jc == column_chunk(2, row))
+            def _():
+                wait_bytes(tok.at[jc, upper], far_sem.at[far, 0])
+                wait_bytes(tok.at[jc, lower], far_sem.at[far, 1])
 
         for r in (2, 1, 3, 0):
 
@@ -261,8 +297,13 @@
         gain = skip_gain[:, lanes]
         gath[j, :, lanes] = (q_scr[...] * (y_scr[...] + gain * s_scr[...])).astype(BF16)
         own = gath.at[j, :, lanes]
-        for peer in (z_next, z_prev, z_far, y_far):
+        for peer in (z_far, z_next, z_prev, y_far):
             remote(own, own, send_sem.at[7], gath_sem.at[block, j], peer).start()
+
+        @pl.when(j >= DIRECT)
+        def _():
+            for peer in diagonals:
+                remote(own, own, send_sem.at[7], gath_sem.at[block, j], peer).start()
 
     def forward(j):
         for r in (1, 3, 2):
@@ -271,8 +312,6 @@
             wait_bytes(there, gath_sem.at[b, j])
             remote(there, there, send_sem.at[7], gath_sem.at[b, j], y_far).start()
 
-    upper, lower = pl.ds(0, HALF), pl.ds(HALF, HALF)
-
     def distance(j):
         return lax.rem(j // 2 - x + 4, 4)
 
@@ -280,6 +319,12 @@
         for r in range(4):
             b = (1 - y_hi) * 4 + r
             wait_bytes(gath.at[j, :, pl.ds(aligned(b, LANES), LANES)], gath_sem.at[b, j])
+
+        @pl.when(j >= DIRECT)
+        def _():
+            for r in (1, 3, 2):
+                b = y_hi * 4 + lax.rem(z + r, 4)
+                wait_bytes(gath.at[j, :, pl.ds(aligned(b, LANES), LANES)], gath_sem.at[b, j])
 
         @pl.when(j == 0)
         def _():
@@ -349,30 +394,42 @@
             remote(o_fin, out.at[own_rows, :], send_sem.at[8], fin_sem.at[0], sibling).start()
             out[own_rows, :] = (o_acc[:, mine] + o_y[:, mine].astype(F32)).astype(BF16)
 
-    def step(i, carry):
-        def stage(lag, body):
-            @pl.when(jnp.logical_and(i >= lag, i < lag + CHUNKS))
-            def _():
-                body(i - lag)
-
-        @pl.when(i == 1)
+    def step(n, carry):
+        def stage(times, body):
+            first_chunk, end_chunk = jnp.int32(0), jnp.int32(0)
+            for time in times:
+                first_chunk = first_chunk + jnp.where(n > time, 1, 0)
+                end_chunk = end_chunk + jnp.where(n >= time, 1, 0)
+
+            def call(j, unused):
+                body(j)
+                return unused
+
+            lax.fori_loop(first_chunk, end_chunk, call, 0)
+
+        @pl.when(n == 2)
         def _():
             wait_bytes(tok.at[near], tok_sem.at[near])
-            for peer in (x_next, x_prev, x_far):
+            relay_tokens(y_lo, 0)
+            for peer in (x_next, x_prev):
                 remote(tok.at[near], tok.at[near], send_sem.at[0], tok_sem.at[near], peer).start()
 
-        stage(0, project)
-        stage(1, lambda k: pass_on(order(k)))
-        stage(2, lambda k: cross(order(k)))
-        stage(4, convolve)
-        stage(5, forward)
-        stage(6, finish)
-        stage(7, o_pass)
-        stage(8, o_cross)
-        stage(9, o_last)
+        @pl.when(n == 6)
+        def _():
+            relay_tokens(1 - y_lo, 1)
+
+        stage(range(0, 16, 2), project)
+        stage(range(1, 17, 2), lambda k: pass_on(order(k)))
+        stage(range(3, 19, 2), lambda k: cross(order(k)))
+        stage(CONVOLVE_AT, convolve)
+        stage([t + 1 for t in CONVOLVE_AT[:DIRECT]], forward)
+        stage(FINISH_AT, finish)
+        stage([t + 1 for t in FINISH_AT], o_pass)
+        stage([t + 2 for t in FINISH_AT], o_cross)
+        stage([t + 3 for t in FINISH_AT], o_last)
         return carry
 
-    lax.fori_loop(0, CHUNKS + 9, step, 0)
+    lax.fori_loop(0, FINISH_AT[-1] + 4, step, 0)
 
     wait_bytes(o_fin, fin_sem.at[0])
     wait_bytes(tok.at[pl.ds(0, 7)], send_sem.at[0])
@@ -429,6 +486,7 @@
         pltpu.VMEM((ROWS, FEATURES), BF16),
         dma((6,)),
         dma((CHUNKS + 1,)),
+        dma((2, 2)),
         dma((4,)),
         dma((1,)),
         dma((2, CHUNKS)),

time: 133 us -> 126 us (0.947)
  Pallas kernels: 131 us -> 124 us
    pallas_call x1, Pallas kernels: 131 us -> 124 us  [local(): pl.pallas_call(kernel, out_shape=jax.ShapeDtypeStruct(tokens.shape, BF16)...]
where the time goes in v3:
time: 126 us
  Pallas kernels  124 us (98%)
  local copies, waits for them, and re-layouts  1.67 us (1%)
    pallas_call x1, Pallas kernels, local(): pl.pallas_call(kernel, out_shape=jax.ShapeDtypeStruct(tokens.shape, BF16)...  124 us

profile of v3, /device:TPU:15, one launch (start us, length us, event | category | flops | bytes accessed | tf_op | source)
XLA Modules:
  0.0 125.9 jit_solution(18210077851742784606)
XLA Ops:
  0.0 124.2 %hyena_block.1 = bf16[256,512]{1,0:T(8,128)(2,1)} custom-call(bf16[256,512]{1,0:T(8,128)(2,1)} %tokens.1, bf16[3,512,1024]{2,1,0:T(8,128)(2,1)} %bitcast.2, f32[16,1024]{1,0:T(8,128)} %residues.1, f32[16,1024]{1,0:T(8,128)} %decay_rates.1, f32[1,1024]{1,0:T(1,128)} %bitcast.3, bf16[1024,512]{1,0:T(8,128)(2,1)} %out_weight.1), custom_call_target="tpu_custom_call" | custom-call | tf_op jit(solution)/shard_map/hyena_block/pallas_call | solution.py:505
  124.2 1.7 %copy.8 = bf16[256,512]{1,0:T(8,128)(2,1)} copy(bf16[256,512]{1,0:T(8,128)(2,1)} %hyena_block.1) | data formatting | bytes 524288

commit v4 on v3

--- a/solution.py
+++ b/solution.py
@@ -13,6 +13,7 @@
 CHUNKS = 8
 ROWS = 128
 HALF = 64
+QUARTER = 32
 LANES = 128
 MODES = 16
 SEGS = 8
@@ -85,11 +86,11 @@
     gath,
     p_out,
     o_relay,
-    o_dir,
-    o_sum,
-    o_acc,
+    o_y_in,
+    o_in,
+    o_sib,
+    o_send,
     o_y,
-    o_fin,
     local_sem,
     tok_sem,
     far_sem,
@@ -102,10 +103,10 @@
     state_sem,
     gath_sem,
     o_relay_sem,
-    o_dir_sem,
-    o_sum_sem,
+    o_y_in_sem,
+    o_in_sem,
+    o_sib_sem,
     o_y_sem,
-    fin_sem,
     send_sem,
 ):
     seq = lax.axis_index("seq")
@@ -131,6 +132,7 @@
     y_near = at(flip_lo=True)
     diagonals = [at(dz=r, flip_hi=True) for r in (2, 1, 3)]
     peers = [sibling, z_next, z_prev, z_far, y_far, x_next, x_prev, y_near, *diagonals]
+    peers += [at(dx=1, flip_core=True), at(dx=3, flip_core=True)]
     block = y_hi * 4 + z
     lanes = pl.ds(aligned(block, LANES), LANES)
 
@@ -334,65 +336,123 @@
         for h in range(2):
             cols = pl.ds(h * FEATURES, FEATURES)
             p_out[j, :, cols] = jnp.dot(gath[j], w_out[h], preferred_element_type=F32).astype(BF16)
+        o_begin(j, 0)
+
+        @pl.when(row_of(j) != y_lo)
+        def _():
+            remote(p_out.at[j, lower], o_y_in.at[j], send_sem.at[8], o_y_in_sem.at[j], y_near).start()
+
+    def row_of(j):
+        return lax.rem(j, 2)
+
+    def quarter(part_index, k):
+        return pl.ds(part_index * HALF + k * QUARTER, QUARTER)
+
+    def own_columns(flip):
+        return pl.ds(aligned(1 - core if flip else core, FEATURES), FEATURES)
+
+    def to_column(src, j, s, kind, k, dx):
+        for flip in (False, True):
+            remote(
+                src.at[:, own_columns(flip)],
+                o_in.at[row_of(j), s, kind, k, core],
+                send_sem.at[8],
+                o_in_sem.at[row_of(j), s],
+                at(dx=dx, flip_core=flip),
+            ).start()
+
+    def o_begin(j, s):
         dx = distance(j)
-        side = lax.rem(j, 2)
 
         @pl.when(dx == 2)
         def _():
-            remote(p_out.at[j, upper], o_relay.at[j], send_sem.at[8], o_relay_sem.at[j], x_next).start()
-            remote(p_out.at[j, lower], o_relay.at[j], send_sem.at[8], o_relay_sem.at[j], x_prev).start()
+            for k, peer in ((0, x_next), (1, x_prev)):
+                remote(
+                    p_out.at[j, quarter(s, k)], o_relay.at[s, j], send_sem.at[8], o_relay_sem.at[s, j], peer
+                ).start()
 
         @pl.when(dx == 1)
         def _():
-            remote(p_out.at[j, lower], o_dir.at[1, side], send_sem.at[8], o_dir_sem.at[1, side], x_next).start()
+            to_column(p_out.at[j, quarter(s, 1)], j, s, 0, 1, 1)
 
         @pl.when(dx == 3)
         def _():
-            remote(p_out.at[j, upper], o_dir.at[0, side], send_sem.at[8], o_dir_sem.at[0, side], x_prev).start()
-
-    def o_pass(j):
+            to_column(p_out.at[j, quarter(s, 0)], j, s, 0, 0, 3)
+
+        @pl.when(dx == 0)
+        def _():
+            rows = pl.ds(s * HALF, HALF)
+            remote(
+                p_out.at[j, rows, own_columns(True)],
+                o_sib.at[row_of(j), s],
+                send_sem.at[8],
+                o_sib_sem.at[row_of(j), s],
+                sibling,
+            ).start()
+
+    def o_pass(j, s):
         dx = distance(j)
-        side = lax.rem(j, 2)
-        for want, rows, k, peer in ((1, upper, 0, x_next), (3, lower, 1, x_prev)):
+        for want, k in ((1, 0), (3, 1)):
 
             @pl.when(dx == want)
             def _():
-                wait_bytes(o_relay.at[j], o_relay_sem.at[j])
-                o_relay[j] = (o_relay[j].astype(F32) + p_out[j, rows, :].astype(F32)).astype(BF16)
-                remote(o_relay.at[j], o_sum.at[k, side], send_sem.at[8], o_sum_sem.at[k, side], peer).start()
-
-    def o_cross(j):
-        side = lax.rem(j, 2)
-
-        @pl.when(distance(j) == 0)
-        def _():
+                wait_bytes(o_relay.at[s, j], o_relay_sem.at[s, j])
+                o_relay[s, j] = (o_relay[s, j].astype(F32) + p_out[j, quarter(s, k), :].astype(F32)).astype(BF16)
+                to_column(o_relay.at[s, j], j, s, 1, k, want)
+
+    def o_total(j, s, k, mine):
+        side = row_of(j)
+        source = core if mine else 1 - core
+        if mine:
+            base = p_out[j, quarter(s, k), own_columns(False)]
+        else:
+            base = o_sib[side, s, pl.ds(k * QUARTER, QUARTER), :]
+        return (
+            base.astype(F32) + o_in[side, s, 0, k, source].astype(F32) + o_in[side, s, 1, k, source].astype(F32)
+        )
+
+    def o_arrived(j, s):
+        wait_bytes(o_in.at[row_of(j), s], o_in_sem.at[row_of(j), s])
+        wait_bytes(o_sib.at[row_of(j), s], o_sib_sem.at[row_of(j), s])
+
+    def o_second(j):
+        @pl.when(row_of(j) == y_lo)
+        def _():
+            wait_bytes(o_y_in.at[j], o_y_in_sem.at[j])
+            p_out[j, lower, :] = (p_out[j, lower, :].astype(F32) + o_y_in[j].astype(F32)).astype(BF16)
+            o_begin(j, 1)
+
+        o_pass(j, 0)
+
+    def o_third(j):
+        @pl.when(row_of(j) == y_lo)
+        def _():
+            o_pass(j, 1)
+
+        @pl.when(jnp.logical_and(distance(j) == 0, row_of(j) != y_lo))
+        def _():
+            o_arrived(j, 0)
             for k in range(2):
-                wait_bytes(o_dir.at[k, side], o_dir_sem.at[k, side])
-                wait_bytes(o_sum.at[k, side], o_sum_sem.at[k, side])
-
-            def total(k, rows):
-                return p_out[j, rows, :].astype(F32) + o_dir[k, side].astype(F32) + o_sum[k, side].astype(F32)
-
-            @pl.when(side == y_lo)
-            def _():
-                for k, rows in ((0, upper), (1, lower)):
-                    o_acc[rows, :] = total(k, rows)
-
-            @pl.when(side != y_lo)
-            def _():
-                for k, rows in ((0, upper), (1, lower)):
-                    p_out[j, rows, :] = total(k, rows).astype(BF16)
-                remote(p_out.at[j], o_y, send_sem.at[8], o_y_sem.at[0], y_near).start()
+                for mine in (True, False):
+                    o_send[core if mine else 1 - core, k] = o_total(j, 0, k, mine).astype(BF16)
+            remote(o_send, o_y, send_sem.at[8], o_y_sem.at[0], y_near).start()
 
     def o_last(j):
         @pl.when(j == tp)
         def _():
-            wait_bytes(o_y, o_y_sem.at[0])
-            mine = pl.ds(aligned(core, FEATURES), FEATURES)
-            theirs = pl.ds(aligned(1 - core, FEATURES), FEATURES)
-            o_fin[...] = (o_acc[:, theirs] + o_y[:, theirs].astype(F32)).astype(BF16)
-            remote(o_fin, out.at[own_rows, :], send_sem.at[8], fin_sem.at[0], sibling).start()
-            out[own_rows, :] = (o_acc[:, mine] + o_y[:, mine].astype(F32)).astype(BF16)
+            o_arrived(j, 0)
+            o_arrived(j, 1)
+            for s in (1, 0):
+                if s == 0:
+                    wait_bytes(o_y, o_y_sem.at[0])
+                for k in range(2):
+                    for mine in (True, False):
+                        source = core if mine else 1 - core
+                        total = o_total(j, s, k, mine)
+                        if s == 0:
+                            total = total + o_y[source, k].astype(F32)
+                        start = source * ROWS + s * HALF + k * QUARTER
+                        out[pl.ds(pl.multiple_of(start, QUARTER), QUARTER), :] = total.astype(BF16)
 
     def step(n, carry):
         def stage(times, body):
@@ -424,14 +484,13 @@
         stage(CONVOLVE_AT, convolve)
         stage([t + 1 for t in CONVOLVE_AT[:DIRECT]], forward)
         stage(FINISH_AT, finish)
-        stage([t + 1 for t in FINISH_AT], o_pass)
-        stage([t + 2 for t in FINISH_AT], o_cross)
+        stage([t + 1 for t in FINISH_AT], o_second)
+        stage([t + 2 for t in FINISH_AT], o_third)
         stage([t + 3 for t in FINISH_AT], o_last)
         return carry
 
     lax.fori_loop(0, FINISH_AT[-1] + 4, step, 0)
 
-    wait_bytes(o_fin, fin_sem.at[0])
     wait_bytes(tok.at[pl.ds(0, 7)], send_sem.at[0])
     wait_bytes(tok.at[0, :, pl.ds(0, FEATURES)], send_sem.at[0])
     wait_bytes(w_in.at[:, own_feat, :], send_sem.at[1])
@@ -448,7 +507,7 @@
 
     wait_bytes(gath.at[pl.ds(0, 7)], send_sem.at[7])
     wait_bytes(p_out.at[pl.ds(0, 7)], send_sem.at[8])
-    wait_bytes(o_fin, send_sem.at[8])
+    wait_bytes(p_out.at[0, pl.ds(0, 3 * QUARTER)], send_sem.at[8])
 
 
 def local(tokens, in_weight, residues, decay_rates, skip_gain, out_weight):
@@ -478,12 +537,12 @@
         pltpu.VMEM((CHUNKS, MODES, LANES), F32),
         pltpu.VMEM((CHUNKS, ROWS, WIDE), BF16),
         pltpu.VMEM((CHUNKS, ROWS, WIDE), BF16),
+        pltpu.VMEM((2, CHUNKS, QUARTER, WIDE), BF16),
         pltpu.VMEM((CHUNKS, HALF, WIDE), BF16),
-        pltpu.VMEM((2, 2, HALF, WIDE), BF16),
-        pltpu.VMEM((2, 2, HALF, WIDE), BF16),
-        pltpu.VMEM((ROWS, WIDE), F32),
-        pltpu.VMEM((ROWS, WIDE), BF16),
-        pltpu.VMEM((ROWS, FEATURES), BF16),
+        pltpu.VMEM((2, 2, 2, 2, 2, QUARTER, FEATURES), BF16),
+        pltpu.VMEM((2, 2, HALF, FEATURES), BF16),
+        pltpu.VMEM((2, 2, QUARTER, FEATURES), BF16),
+        pltpu.VMEM((2, 2, QUARTER, FEATURES), BF16),
         dma((6,)),
         dma((CHUNKS + 1,)),
         dma((2, 2)),
@@ -495,10 +554,10 @@
         dma((CHUNKS,)),
         dma((CHUNKS + 1,)),
         dma((8, CHUNKS)),
+        dma((2, CHUNKS)),
         dma((CHUNKS,)),
         dma((2, 2)),
         dma((2, 2)),
-        dma((1,)),
         dma((1,)),
         dma((9,)),
     ]

time: 126 us -> 116 us (0.921)
  Pallas kernels: 124 us -> 114 us
    pallas_call x1, Pallas kernels: 124 us -> 114 us  [local(): pl.pallas_call(kernel, out_shape=jax.ShapeDtypeStruct(tokens.shape, BF16)...]
where the time goes in v4:
time: 116 us
  Pallas kernels  114 us (98%)
  local copies, waits for them, and re-layouts  1.67 us (1%)
    pallas_call x1, Pallas kernels, local(): pl.pallas_call(kernel, out_shape=jax.ShapeDtypeStruct(tokens.shape, BF16)...  114 us

profile of v4, /device:TPU:15, one launch (start us, length us, event | category | flops | bytes accessed | tf_op | source)
XLA Modules:
  0.0 115.6 jit_solution(6921372399718432594)
XLA Ops:
  0.0 113.9 %hyena_block.1 = bf16[256,512]{1,0:T(8,128)(2,1)} custom-call(bf16[256,512]{1,0:T(8,128)(2,1)} %tokens.1, bf16[3,512,1024]{2,1,0:T(8,128)(2,1)} %bitcast.2, f32[16,1024]{1,0:T(8,128)} %residues.1, f32[16,1024]{1,0:T(8,128)} %decay_rates.1, f32[1,1024]{1,0:T(1,128)} %bitcast.3, bf16[1024,512]{1,0:T(8,128)(2,1)} %out_weight.1), custom_call_target="tpu_custom_call" | custom-call | tf_op jit(solution)/shard_map/hyena_block/pallas_call | solution.py:564
  113.9 1.7 %copy.8 = bf16[256,512]{1,0:T(8,128)(2,1)} copy(bf16[256,512]{1,0:T(8,128)(2,1)} %hyena_block.1) | data formatting | bytes 524288

commit v5 on v4

--- a/solution.py
+++ b/solution.py
@@ -21,9 +21,14 @@
 QKV = 3 * LANES
 FEATURES = 512
 WIDE = 1024
-DIRECT = 6
-CONVOLVE_AT = (12, 12, 13, 14, 15, 16, 18, 19)
-FINISH_AT = (14, 14, 15, 16, 17, 18, 19, 20)
+DIRECT = 5
+SPLIT = 6
+EARLY = 7
+LATE = CHUNKS - EARLY
+PROJECT_LATE_AT = (9,)
+START_LATE_AT = (13,)
+CONVOLVE_AT = (12, 12, 13, 14, 14, 16, 16, 17)
+FINISH_AT = (14, 14, 15, 16, 16, 17, 17, 18)
 CHUNK_ORDERS = (
     (0, 1, 2, 3, 4, 5, 6, 7),
     (1, 0, 3, 2, 4, 5, 6, 7),
@@ -73,6 +78,10 @@
     summed,
     y_send,
     y_recv,
+    crossed,
+    relay_l,
+    direct_l,
+    summed_l,
     s_scr,
     y_scr,
     q_scr,
@@ -100,6 +109,10 @@
     direct_sem,
     summed_sem,
     y_sem,
+    crossed_sem,
+    relay_l_sem,
+    direct_l_sem,
+    summed_l_sem,
     state_sem,
     gath_sem,
     o_relay_sem,
@@ -188,6 +201,10 @@
     def _():
         state_in[0] = jnp.zeros((MODES, LANES), F32)
 
+    @pl.when(tp >= SPLIT)
+    def _():
+        o_y[1] = jnp.zeros((2, 2, QUARTER, FEATURES), BF16)
+
     upper, lower = pl.ds(0, HALF), pl.ds(HALF, HALF)
     near = x * 2 + 1 - y_lo
     code = jnp.int32(ORDERS[0])
@@ -216,15 +233,17 @@
 
     first, second = pl.ds(0, QKV), pl.ds(QKV, QKV)
 
-    def project(i):
-        jc = order(i)
-
+    def await_tokens(jc):
         for far, row in ((0, y_lo), (1, 1 - y_lo)):
 
             @pl.when(jc == column_chunk(2, row))
             def _():
                 wait_bytes(tok.at[jc, upper], far_sem.at[far, 0])
                 wait_bytes(tok.at[jc, lower], far_sem.at[far, 1])
+
+    def project(i):
+        jc = order(i)
+        await_tokens(jc)
 
         for r in (2, 1, 3, 0):
 
@@ -241,6 +260,40 @@
             elif r == 3:
                 remote(part.at[jc, 3, :, first], direct.at[0, jc], send_sem.at[3], direct_sem.at[0, jc], z_prev).start()
 
+    def project_late(u):
+        jc = order(EARLY + u)
+        await_tokens(jc)
+        theirs = pl.ds(aligned(1 - y_hi, QKV), QKV)
+        for r in (2, 1, 3, 0):
+            multiply(jc, r)
+            remote(part.at[jc, r, :, theirs], crossed.at[u, r], send_sem.at[9], crossed_sem.at[u], y_far).start()
+
+    def start_late(u):
+        jc = order(EARLY + u)
+        mine = pl.ds(aligned(y_hi, QKV), QKV)
+        wait_bytes(crossed.at[u], crossed_sem.at[u])
+        for r in (2, 1, 3, 0):
+            crossed[u, r] = (crossed[u, r].astype(F32) + part[jc, r, :, mine].astype(F32)).astype(BF16)
+            if r == 2:
+                for k, rows, peer in ((0, upper, z_next), (1, lower, z_prev)):
+                    remote(
+                        crossed.at[u, 2, rows], relay_l.at[u, k], send_sem.at[10], relay_l_sem.at[u, k], peer
+                    ).start()
+            elif r == 1:
+                remote(
+                    crossed.at[u, 1, lower], direct_l.at[u, 1], send_sem.at[10], direct_l_sem.at[u, 1], z_next
+                ).start()
+            elif r == 3:
+                remote(
+                    crossed.at[u, 3, upper], direct_l.at[u, 0], send_sem.at[10], direct_l_sem.at[u, 0], z_prev
+                ).start()
+
+    def pass_late(u):
+        for k, r, rows, peer in ((0, 1, upper, z_next), (1, 3, lower, z_prev)):
+            wait_bytes(relay_l.at[u, k], relay_l_sem.at[u, k])
+            relay_l[u, k] = (relay_l[u, k].astype(F32) + crossed[u, r, rows].astype(F32)).astype(BF16)
+            remote(relay_l.at[u, k], summed_l.at[u, k], send_sem.at[10], summed_l_sem.at[u, k], peer).start()
+
     def pass_on(jc):
         for k, r, cols, peer in ((0, 1, first, z_next), (1, 3, second, z_prev)):
             wait_bytes(relay.at[k, jc], relay_sem.at[k, jc])
@@ -259,10 +312,31 @@
         remote(y_send.at[jc], y_recv.at[jc], send_sem.at[5], y_sem.at[jc], y_far).start()
 
     def convolve(j):
-        wait_bytes(y_recv.at[j], y_sem.at[j])
-        total = gather_half(j, y_hi) + y_recv[j].astype(F32)
-        q_scr[...] = total[:, :LANES]
-        s_scr[...] = total[:, LANES : 2 * LANES] * total[:, 2 * LANES :]
+        def keep(rows, total):
+            q_scr[rows, :] = total[:, :LANES]
+            s_scr[rows, :] = total[:, LANES : 2 * LANES] * total[:, 2 * LANES :]
+
+        late = jnp.int32(-1)
+        for u in range(LATE):
+            late = jnp.where(order(EARLY + u) == j, u, late)
+
+        @pl.when(late < 0)
+        def _():
+            wait_bytes(y_recv.at[j], y_sem.at[j])
+            keep(pl.ds(0, ROWS), gather_half(j, y_hi) + y_recv[j].astype(F32))
+
+        @pl.when(late >= 0)
+        def _():
+            for k, rows in ((0, upper), (1, lower)):
+                wait_bytes(direct_l.at[late, k], direct_l_sem.at[late, k])
+                wait_bytes(summed_l.at[late, k], summed_l_sem.at[late, k])
+                keep(
+                    rows,
+                    crossed[late, 0, rows].astype(F32)
+                    + direct_l[late, k].astype(F32)
+                    + summed_l[late, k].astype(F32),
+                )
+
         decay = [decay_b[m] for m in range(MODES)]
         held = [jnp.zeros((SEGS, LANES), F32)] * MODES
         for i in range(STEPS):
@@ -338,7 +412,11 @@
             p_out[j, :, cols] = jnp.dot(gath[j], w_out[h], preferred_element_type=F32).astype(BF16)
         o_begin(j, 0)
 
-        @pl.when(row_of(j) != y_lo)
+        @pl.when(j < SPLIT)
+        def _():
+            o_begin(j, 1)
+
+        @pl.when(jnp.logical_and(j >= SPLIT, row_of(j) != y_lo))
         def _():
             remote(p_out.at[j, lower], o_y_in.at[j], send_sem.at[8], o_y_in_sem.at[j], y_near).start()
 
@@ -416,7 +494,7 @@
         wait_bytes(o_sib.at[row_of(j), s], o_sib_sem.at[row_of(j), s])
 
     def o_second(j):
-        @pl.when(row_of(j) == y_lo)
+        @pl.when(jnp.logical_and(j >= SPLIT, row_of(j) == y_lo))
         def _():
             wait_bytes(o_y_in.at[j], o_y_in_sem.at[j])
             p_out[j, lower, :] = (p_out[j, lower, :].astype(F32) + o_y_in[j].astype(F32)).astype(BF16)
@@ -424,33 +502,47 @@
 
         o_pass(j, 0)
 
+        @pl.when(j < SPLIT)
+        def _():
+            o_pass(j, 1)
+
+    def o_over(j, s):
+        o_arrived(j, s)
+        for k in range(2):
+            for mine in (True, False):
+                o_send[s, core if mine else 1 - core, k] = o_total(j, s, k, mine).astype(BF16)
+        remote(o_send.at[s], o_y.at[s], send_sem.at[8], o_y_sem.at[s], y_near).start()
+
     def o_third(j):
-        @pl.when(row_of(j) == y_lo)
+        @pl.when(jnp.logical_and(j >= SPLIT, row_of(j) == y_lo))
         def _():
             o_pass(j, 1)
 
         @pl.when(jnp.logical_and(distance(j) == 0, row_of(j) != y_lo))
         def _():
-            o_arrived(j, 0)
-            for k in range(2):
-                for mine in (True, False):
-                    o_send[core if mine else 1 - core, k] = o_total(j, 0, k, mine).astype(BF16)
-            remote(o_send, o_y, send_sem.at[8], o_y_sem.at[0], y_near).start()
+            o_over(j, 0)
+
+            @pl.when(j < SPLIT)
+            def _():
+                o_over(j, 1)
 
     def o_last(j):
         @pl.when(j == tp)
         def _():
-            o_arrived(j, 0)
-            o_arrived(j, 1)
             for s in (1, 0):
+                o_arrived(j, s)
                 if s == 0:
-                    wait_bytes(o_y, o_y_sem.at[0])
+                    wait_bytes(o_y.at[0], o_y_sem.at[0])
+                else:
+
+                    @pl.when(j < SPLIT)
+                    def _():
+                        wait_bytes(o_y.at[1], o_y_sem.at[1])
+
                 for k in range(2):
                     for mine in (True, False):
                         source = core if mine else 1 - core
-                        total = o_total(j, s, k, mine)
-                        if s == 0:
-                            total = total + o_y[source, k].astype(F32)
+                        total = o_total(j, s, k, mine) + o_y[s, source, k].astype(F32)
                         start = source * ROWS + s * HALF + k * QUARTER
                         out[pl.ds(pl.multiple_of(start, QUARTER), QUARTER), :] = total.astype(BF16)
 
@@ -478,9 +570,12 @@
         def _():
             relay_tokens(1 - y_lo, 1)
 
-        stage(range(0, 16, 2), project)
-        stage(range(1, 17, 2), lambda k: pass_on(order(k)))
-        stage(range(3, 19, 2), lambda k: cross(order(k)))
+        stage(range(0, 2 * EARLY, 2), project)
+        stage(START_LATE_AT, start_late)
+        stage(range(1, 2 * EARLY, 2), lambda k: pass_on(order(k)))
+        stage([t + 1 for t in START_LATE_AT], pass_late)
+        stage(range(3, 2 * EARLY + 2, 2), lambda k: cross(order(k)))
+        stage(PROJECT_LATE_AT, project_late)
         stage(CONVOLVE_AT, convolve)
         stage([t + 1 for t in CONVOLVE_AT[:DIRECT]], forward)
         stage(FINISH_AT, finish)
@@ -495,10 +590,14 @@
     wait_bytes(tok.at[0, :, pl.ds(0, FEATURES)], send_sem.at[0])
     wait_bytes(w_in.at[:, own_feat, :], send_sem.at[1])
     wait_bytes(out_weight, send_sem.at[1])
-    wait_bytes(relay, send_sem.at[2])
-    wait_bytes(direct, send_sem.at[3])
-    wait_bytes(summed, send_sem.at[4])
-    wait_bytes(y_recv, send_sem.at[5])
+    early = pl.ds(0, EARLY)
+    wait_bytes(relay.at[:, early], send_sem.at[2])
+    wait_bytes(direct.at[:, early], send_sem.at[3])
+    wait_bytes(summed.at[:, early], send_sem.at[4])
+    wait_bytes(y_recv.at[early], send_sem.at[5])
+    wait_bytes(crossed, send_sem.at[9])
+    for arrived in (relay_l, direct_l, summed_l):
+        wait_bytes(arrived, send_sem.at[10])
     wait_bytes(state_out.at[pl.ds(0, CHUNKS - 1)], send_sem.at[6])
 
     @pl.when(core == 0)
@@ -508,6 +607,10 @@
     wait_bytes(gath.at[pl.ds(0, 7)], send_sem.at[7])
     wait_bytes(p_out.at[pl.ds(0, 7)], send_sem.at[8])
     wait_bytes(p_out.at[0, pl.ds(0, 3 * QUARTER)], send_sem.at[8])
+
+    @pl.when(tp < SPLIT)
+    def _():
+        wait_bytes(p_out.at[0, pl.ds(0, QUARTER)], send_sem.at[8])
 
 
 def local(tokens, in_weight, residues, decay_rates, skip_gain, out_weight):
@@ -525,6 +628,10 @@
         pltpu.VMEM((2, CHUNKS, ROWS, QKV), BF16),
         pltpu.VMEM((CHUNKS, ROWS, QKV), BF16),
         pltpu.VMEM((CHUNKS, ROWS, QKV), BF16),
+        pltpu.VMEM((LATE, 4, ROWS, QKV), BF16),
+        pltpu.VMEM((LATE, 2, HALF, QKV), BF16),
+        pltpu.VMEM((LATE, 2, HALF, QKV), BF16),
+        pltpu.VMEM((LATE, 2, HALF, QKV), BF16),
         pltpu.VMEM((ROWS, LANES), F32),
         pltpu.VMEM((ROWS, LANES), F32),
         pltpu.VMEM((ROWS, LANES), F32),
@@ -541,8 +648,8 @@
         pltpu.VMEM((CHUNKS, HALF, WIDE), BF16),
         pltpu.VMEM((2, 2, 2, 2, 2, QUARTER, FEATURES), BF16),
         pltpu.VMEM((2, 2, HALF, FEATURES), BF16),
-        pltpu.VMEM((2, 2, QUARTER, FEATURES), BF16),
-        pltpu.VMEM((2, 2, QUARTER, FEATURES), BF16),
+        pltpu.VMEM((2, 2, 2, QUARTER, FEATURES), BF16),
+        pltpu.VMEM((2, 2, 2, QUARTER, FEATURES), BF16),
         dma((6,)),
         dma((CHUNKS + 1,)),
         dma((2, 2)),
@@ -552,14 +659,18 @@
         dma((2, CHUNKS)),
         dma((2, CHUNKS)),
         dma((CHUNKS,)),
+        dma((LATE,)),
+        dma((LATE, 2)),
+        dma((LATE, 2)),
+        dma((LATE, 2)),
         dma((CHUNKS + 1,)),
         dma((8, CHUNKS)),
         dma((2, CHUNKS)),
         dma((CHUNKS,)),
         dma((2, 2)),
         dma((2, 2)),
-        dma((1,)),
-        dma((9,)),
+        dma((2,)),
+        dma((11,)),
     ]
     return pl.pallas_call(
         kernel,

time: 116 us -> 111 us (0.957)
  Pallas kernels: 114 us -> 109 us
    pallas_call x1, Pallas kernels: 114 us -> 109 us  [local(): pl.pallas_call(kernel, out_shape=jax.ShapeDtypeStruct(tokens.shape, BF16)...]
where the time goes in v5:
time: 111 us
  Pallas kernels  109 us (98%)
  local copies, waits for them, and re-layouts  1.67 us (2%)
    pallas_call x1, Pallas kernels, local(): pl.pallas_call(kernel, out_shape=jax.ShapeDtypeStruct(tokens.shape, BF16)...  109 us

profile of v5, /device:TPU:15, one launch (start us, length us, event | category | flops | bytes accessed | tf_op | source)
XLA Modules:
  0.0 111.0 jit_solution(9551652829713568432)
XLA Ops:
  0.0 109.3 %hyena_block.1 = bf16[256,512]{1,0:T(8,128)(2,1)} custom-call(bf16[256,512]{1,0:T(8,128)(2,1)} %tokens.1, bf16[3,512,1024]{2,1,0:T(8,128)(2,1)} %bitcast.2, f32[16,1024]{1,0:T(8,128)} %residues.1, f32[16,1024]{1,0:T(8,128)} %decay_rates.1, f32[1,1024]{1,0:T(1,128)} %bitcast.3, bf16[1024,512]{1,0:T(8,128)(2,1)} %out_weight.1), custom_call_target="tpu_custom_call" | custom-call | tf_op jit(solution)/shard_map/hyena_block/pallas_call | solution.py:675
  109.3 1.7 %copy.8 = bf16[256,512]{1,0:T(8,128)(2,1)} copy(bf16[256,512]{1,0:T(8,128)(2,1)} %hyena_block.1) | data formatting | bytes 524288

commit v6 on v5

--- a/solution.py
+++ b/solution.py
@@ -27,8 +27,8 @@
 LATE = CHUNKS - EARLY
 PROJECT_LATE_AT = (9,)
 START_LATE_AT = (13,)
-CONVOLVE_AT = (12, 12, 13, 14, 14, 16, 16, 17)
-FINISH_AT = (14, 14, 15, 16, 16, 17, 17, 18)
+CONVOLVE_AT = (12, 12, 13, 14, 14, 16, 16, 16)
+FINISH_AT = (15, 15, 15, 16, 16, 17, 17, 17)
 CHUNK_ORDERS = (
     (0, 1, 2, 3, 4, 5, 6, 7),
     (1, 0, 3, 2, 4, 5, 6, 7),
@@ -64,11 +64,14 @@
 def kernel(
     tokens,
     in_weight,
+    residues_in,
+    decay_rates_in,
+    skip_gain_in,
+    out_weight,
+    out,
     residues,
     decay_rates,
     skip_gain,
-    out_weight,
-    out,
     tok,
     w_in,
     w_out,
@@ -173,6 +176,14 @@
                     local_sem.at[1 + r],
                 ).start()
     pltpu.make_async_copy(out_weight, w_out.at[core], local_sem.at[5]).start()
+    small = [
+        pltpu.make_async_copy(whole.at[:, lanes], piece, local_sem.at[6 + k])
+        for k, (whole, piece) in enumerate(
+            ((residues_in, residues), (decay_rates_in, decay_rates), (skip_gain_in, skip_gain))
+        )
+    ]
+    for copy in small:
+        copy.start()
 
     pl.semaphore_wait(barrier, len(peers))
     remote(tokens.at[other_rows, :], tok.at[tp, :, own_feat], send_sem.at[0], tok_sem.at[CHUNKS], sibling).start()
@@ -187,12 +198,14 @@
         remote(own_weight(r), own_weight(r), send_sem.at[1], w_sem.at[r], sibling).start()
     remote(out_weight, w_out.at[core], send_sem.at[1], wo_sem.at[0], sibling).start()
 
+    for copy in small:
+        copy.wait()
     seg_index = lax.broadcasted_iota(jnp.int32, (SEGS, LANES), 0)
     seg_next = (seg_index + 1).astype(F32) * float(STEPS)
     for m in range(MODES):
-        rate = jnp.broadcast_to(decay_rates[pl.ds(m, 1), lanes], (SEGS, LANES))
+        rate = jnp.broadcast_to(decay_rates[pl.ds(m, 1), :], (SEGS, LANES))
         decay_b[m] = jnp.exp(-rate)
-        res_b[m] = jnp.broadcast_to(residues[pl.ds(m, 1), lanes], (SEGS, LANES))
+        res_b[m] = jnp.broadcast_to(residues[pl.ds(m, 1), :], (SEGS, LANES))
         seg_b[m] = jnp.exp(-rate * seg_next)
         for k in range(3):
             scan_b[k, m] = jnp.where(seg_index >= (1 << k), jnp.exp(-rate * float(STEPS << k)), 0.0)
@@ -370,7 +383,7 @@
             while len(terms) > 1:
                 terms = [terms[k] + terms[k + 1] for k in range(0, len(terms), 2)]
             y_scr[pl.ds(i, SEGS, stride=STEPS), :] = terms[0]
-        gain = skip_gain[:, lanes]
+        gain = skip_gain[...]
         gath[j, :, lanes] = (q_scr[...] * (y_scr[...] + gain * s_scr[...])).astype(BF16)
         own = gath.at[j, :, lanes]
         for peer in (z_far, z_next, z_prev, y_far):
@@ -619,6 +632,9 @@
     anywhere = pl.BlockSpec(memory_space=pl.ANY)
     dma = pltpu.SemaphoreType.DMA
     scratch = [
+        pltpu.VMEM((MODES, LANES), F32),
+        pltpu.VMEM((MODES, LANES), F32),
+        pltpu.VMEM((1, LANES), F32),
         pltpu.VMEM((CHUNKS, ROWS, WIDE), BF16),
         pltpu.VMEM((4, WIDE, 2 * QKV), BF16),
         pltpu.VMEM((2, WIDE, FEATURES), BF16),
@@ -650,7 +666,7 @@
         pltpu.VMEM((2, 2, HALF, FEATURES), BF16),
         pltpu.VMEM((2, 2, 2, QUARTER, FEATURES), BF16),
         pltpu.VMEM((2, 2, 2, QUARTER, FEATURES), BF16),
-        dma((6,)),
+        dma((9,)),
         dma((CHUNKS + 1,)),
         dma((2, 2)),
         dma((4,)),
@@ -674,8 +690,8 @@
     ]
     return pl.pallas_call(
         kernel,
-        out_shape=jax.ShapeDtypeStruct(tokens.shape, BF16),
-        in_specs=[anywhere, anywhere, vmem, vmem, vmem, anywhere],
+        out_shape=pltpu.VMEM(tokens.shape, BF16),
+        in_specs=[anywhere] * 6,
         out_specs=vmem,
         scratch_shapes=scratch,
         compiler_params=pltpu.CompilerParams(

time: 111 us -> 103 us (0.928)
  Pallas kernels: 109 us -> 102 us
    pallas_call x1, Pallas kernels: 109 us -> 102 us  [local(): pl.pallas_call(kernel, out_shape=pltpu.VMEM(tokens.shape, BF16), in_specs...]
where the time goes in v6:
time: 103 us
  Pallas kernels  102 us (99%)
    pallas_call x1, Pallas kernels, local(): pl.pallas_call(kernel, out_shape=pltpu.VMEM(tokens.shape, BF16), in_specs...  102 us

profile of v6, /device:TPU:15, one launch (start us, length us, event | category | flops | bytes accessed | tf_op | source)
XLA Modules:
  0.0 102.7 jit_solution(7822846752509739650)
XLA Ops:
  0.0 102.0 %hyena_block.1 = bf16[256,512]{1,0:T(8,128)(2,1)S(1)} custom-call(bf16[256,512]{1,0:T(8,128)(2,1)} %tokens.1, bf16[3,512,1024]{2,1,0:T(8,128)(2,1)} %bitcast.2, f32[16,1024]{1,0:T(8,128)} %residues_in.1, f32[16,1024]{1,0:T(8,128)} %decay_rates_in.1, f32[1,1024]{1,0:T(1,128)} %bitcast.3, bf16[1024,512]{1,0:T(8,128)(2,1)} %out_weight.1), custom_call_target="tpu_custom_call" | custom-call | tf_op jit(solution)/shard_map/hyena_block/pallas_call | solution.py:691
  102.0 0.7 copy.8

commit v7 on v6

--- a/solution.py
+++ b/solution.py
@@ -22,12 +22,13 @@
 FEATURES = 512
 WIDE = 1024
 DIRECT = 5
-SPLIT = 6
+SPLIT = 5
 EARLY = 7
 LATE = CHUNKS - EARLY
-PROJECT_LATE_AT = (9,)
-START_LATE_AT = (13,)
+PROJECT_LATE_AT = (8,)
+START_LATE_AT = (14,)
 CONVOLVE_AT = (12, 12, 13, 14, 14, 16, 16, 16)
+FORWARD_AT = (13, 13, 14, 15, 15)
 FINISH_AT = (15, 15, 15, 16, 16, 17, 17, 17)
 CHUNK_ORDERS = (
     (0, 1, 2, 3, 4, 5, 6, 7),
@@ -95,6 +96,9 @@
     ends,
     state_in,
     state_out,
+    carry,
+    start,
+    span,
     gath,
     p_out,
     o_relay,
@@ -210,9 +214,9 @@
         for k in range(3):
             scan_b[k, m] = jnp.where(seg_index >= (1 << k), jnp.exp(-rate * float(STEPS << k)), 0.0)
 
-    @pl.when(core == 0)
-    def _():
-        state_in[0] = jnp.zeros((MODES, LANES), F32)
+    carry[...] = jnp.zeros((MODES, LANES), F32)
+    start[...] = jnp.zeros((MODES, LANES), F32)
+    span[...] = jnp.exp(-decay_rates[...] * float(ROWS))
 
     @pl.when(tp >= SPLIT)
     def _():
@@ -360,20 +364,30 @@
             for k in range(3):
                 total = total + scan_b[k, m] * pltpu.roll(total, 1 << k, 0)
             ends[m] = total
-
-        @pl.when(jnp.logical_or(core == 1, j > 0))
+            state_out[j, pl.ds(m, 1), :] = total[SEGS - 1 :, :]
+
+        @pl.when(jnp.logical_or(core == 0, j < CHUNKS - 1))
+        def _():
+            remote(state_out.at[j], state_in.at[j], send_sem.at[6], state_sem.at[j], sibling).start()
+
+        @pl.when(core == 1)
         def _():
             wait_bytes(state_in.at[j], state_sem.at[j])
+            before = span[...] * carry[...] + state_in[j]
+            start[...] = before
+            carry[...] = span[...] * before + state_out[j]
+
+        @pl.when(jnp.logical_and(core == 0, j > 0))
+        def _():
+            wait_bytes(state_in.at[j - 1], state_sem.at[j - 1])
+            before = span[...] * (span[...] * carry[...] + state_out[j - 1]) + state_in[j - 1]
+            start[...] = before
+            carry[...] = before
 
         for m in range(MODES):
-            before = jnp.broadcast_to(state_in[j, pl.ds(m, 1), :], (SEGS, LANES))
+            before = jnp.broadcast_to(start[pl.ds(m, 1), :], (SEGS, LANES))
             full = ends[m] + seg_b[m] * before
-            state_out[j, pl.ds(m, 1), :] = full[SEGS - 1 :, :]
             ends[m] = jnp.where(seg_index == 0, before, pltpu.roll(full, 1, 0))
-
-        @pl.when(jnp.logical_or(core == 0, j < CHUNKS - 1))
-        def _():
-            remote(state_out.at[j], state_in.at[j + core], send_sem.at[6], state_sem.at[j + core], sibling).start()
 
         held = [ends[m] for m in range(MODES)]
         for i in range(STEPS):
@@ -590,7 +604,7 @@
         stage(range(3, 2 * EARLY + 2, 2), lambda k: cross(order(k)))
         stage(PROJECT_LATE_AT, project_late)
         stage(CONVOLVE_AT, convolve)
-        stage([t + 1 for t in CONVOLVE_AT[:DIRECT]], forward)
+        stage(FORWARD_AT, forward)
         stage(FINISH_AT, finish)
         stage([t + 1 for t in FINISH_AT], o_second)
         stage([t + 2 for t in FINISH_AT], o_third)
@@ -621,7 +635,7 @@
     wait_bytes(p_out.at[pl.ds(0, 7)], send_sem.at[8])
     wait_bytes(p_out.at[0, pl.ds(0, 3 * QUARTER)], send_sem.at[8])
 
-    @pl.when(tp < SPLIT)
+    @pl.when(near < SPLIT)
     def _():
         wait_bytes(p_out.at[0, pl.ds(0, QUARTER)], send_sem.at[8])
 
@@ -658,6 +672,9 @@
         pltpu.VMEM((MODES, SEGS, LANES), F32),
         pltpu.VMEM((CHUNKS + 1, MODES, LANES), F32),
         pltpu.VMEM((CHUNKS, MODES, LANES), F32),
+        pltpu.VMEM((MODES, LANES), F32),
+        pltpu.VMEM((MODES, LANES), F32),
+        pltpu.VMEM((MODES, LANES), F32),
         pltpu.VMEM((CHUNKS, ROWS, WIDE), BF16),
         pltpu.VMEM((CHUNKS, ROWS, WIDE), BF16),
         pltpu.VMEM((2, CHUNKS, QUARTER, WIDE), BF16),

time: 103 us -> 100 us (0.971)
  Pallas kernels: 102 us -> 99.1 us
    pallas_call x1, Pallas kernels: 102 us -> 99.1 us  [local(): pl.pallas_call(kernel, out_shape=pltpu.VMEM(tokens.shape, BF16), in_specs...]
where the time goes in v7:
time: 100 us; the launch traced here: 99.8 us
  Pallas kernels  99.1 us (99%)
    pallas_call x1, Pallas kernels, local(): pl.pallas_call(kernel, out_shape=pltpu.VMEM(tokens.shape, BF16), in_specs...  99.1 us

profile of v7, /device:TPU:15, one launch (start us, length us, event | category | flops | bytes accessed | tf_op | source)
XLA Modules:
  0.0 99.8 jit_solution(7420095996093431915)
XLA Ops:
  0.0 99.1 %hyena_block.1 = bf16[256,512]{1,0:T(8,128)(2,1)S(1)} custom-call(bf16[256,512]{1,0:T(8,128)(2,1)} %tokens.1, bf16[3,512,1024]{2,1,0:T(8,128)(2,1)} %bitcast.2, f32[16,1024]{1,0:T(8,128)} %residues_in.1, f32[16,1024]{1,0:T(8,128)} %decay_rates_in.1, f32[1,1024]{1,0:T(1,128)} %bitcast.3, bf16[1024,512]{1,0:T(8,128)(2,1)} %out_weight.1), custom_call_target="tpu_custom_call" | custom-call | tf_op jit(solution)/shard_map/hyena_block/pallas_call | solution.py:708
  99.1 0.7 copy.8

commit v8 on v7

--- a/solution.py
+++ b/solution.py
@@ -400,13 +400,13 @@
         gain = skip_gain[...]
         gath[j, :, lanes] = (q_scr[...] * (y_scr[...] + gain * s_scr[...])).astype(BF16)
         own = gath.at[j, :, lanes]
+        @pl.when(j >= DIRECT)
+        def _():
+            for peer in diagonals:
+                remote(own, own, send_sem.at[7], gath_sem.at[block, j], peer).start()
+
         for peer in (z_far, z_next, z_prev, y_far):
             remote(own, own, send_sem.at[7], gath_sem.at[block, j], peer).start()
-
-        @pl.when(j >= DIRECT)
-        def _():
-            for peer in diagonals:
-                remote(own, own, send_sem.at[7], gath_sem.at[block, j], peer).start()
 
     def forward(j):
         for r in (1, 3, 2):
@@ -520,18 +520,19 @@
         wait_bytes(o_in.at[row_of(j), s], o_in_sem.at[row_of(j), s])
         wait_bytes(o_sib.at[row_of(j), s], o_sib_sem.at[row_of(j), s])
 
-    def o_second(j):
+    def o_second_x(j):
+        o_pass(j, 0)
+
+        @pl.when(j < SPLIT)
+        def _():
+            o_pass(j, 1)
+
+    def o_second_y(j):
         @pl.when(jnp.logical_and(j >= SPLIT, row_of(j) == y_lo))
         def _():
             wait_bytes(o_y_in.at[j], o_y_in_sem.at[j])
             p_out[j, lower, :] = (p_out[j, lower, :].astype(F32) + o_y_in[j].astype(F32)).astype(BF16)
             o_begin(j, 1)
-
-        o_pass(j, 0)
-
-        @pl.when(j < SPLIT)
-        def _():
-            o_pass(j, 1)
 
     def o_over(j, s):
         o_arrived(j, s)
@@ -540,11 +541,12 @@
                 o_send[s, core if mine else 1 - core, k] = o_total(j, s, k, mine).astype(BF16)
         remote(o_send.at[s], o_y.at[s], send_sem.at[8], o_y_sem.at[s], y_near).start()
 
-    def o_third(j):
+    def o_third_x(j):
         @pl.when(jnp.logical_and(j >= SPLIT, row_of(j) == y_lo))
         def _():
             o_pass(j, 1)
 
+    def o_third_y(j):
         @pl.when(jnp.logical_and(distance(j) == 0, row_of(j) != y_lo))
         def _():
             o_over(j, 0)
@@ -600,14 +602,16 @@
         stage(range(0, 2 * EARLY, 2), project)
         stage(START_LATE_AT, start_late)
         stage(range(1, 2 * EARLY, 2), lambda k: pass_on(order(k)))
+        stage(range(3, 2 * EARLY + 2, 2), lambda k: cross(order(k)))
         stage([t + 1 for t in START_LATE_AT], pass_late)
-        stage(range(3, 2 * EARLY + 2, 2), lambda k: cross(order(k)))
         stage(PROJECT_LATE_AT, project_late)
         stage(CONVOLVE_AT, convolve)
         stage(FORWARD_AT, forward)
         stage(FINISH_AT, finish)
-        stage([t + 1 for t in FINISH_AT], o_second)
-        stage([t + 2 for t in FINISH_AT], o_third)
+        stage([t + 1 for t in FINISH_AT], o_second_x)
+        stage([t + 1 for t in FINISH_AT], o_second_y)
+        stage([t + 2 for t in FINISH_AT], o_third_x)
+        stage([t + 2 for t in FINISH_AT], o_third_y)
         stage([t + 3 for t in FINISH_AT], o_last)
         return carry
 

time: 100 us -> 99.7 us (level)
  no operation moved by 1% of the time
where the time goes in v8:
time: 99.7 us; the launch traced here: 99.6 us
  Pallas kernels  98.8 us (99%)
    pallas_call x1, Pallas kernels, local(): pl.pallas_call(kernel, out_shape=pltpu.VMEM(tokens.shape, BF16), in_specs...  98.8 us

profile of v8, /device:TPU:15, one launch (start us, length us, event | category | flops | bytes accessed | tf_op | source)
XLA Modules:
  0.0 99.6 jit_solution(16451341616167163366)
XLA Ops:
  0.0 98.8 %hyena_block.1 = bf16[256,512]{1,0:T(8,128)(2,1)S(1)} custom-call(bf16[256,512]{1,0:T(8,128)(2,1)} %tokens.1, bf16[3,512,1024]{2,1,0:T(8,128)(2,1)} %bitcast.2, f32[16,1024]{1,0:T(8,128)} %residues_in.1, f32[16,1024]{1,0:T(8,128)} %decay_rates_in.1, f32[1,1024]{1,0:T(1,128)} %bitcast.3, bf16[1024,512]{1,0:T(8,128)(2,1)} %out_weight.1), custom_call_target="tpu_custom_call" | custom-call | tf_op jit(solution)/shard_map/hyena_block/pallas_call | solution.py:712
  98.9 0.7 copy.8

commit v9 on v8

--- a/solution.py
+++ b/solution.py
@@ -192,7 +192,9 @@
     pl.semaphore_wait(barrier, len(peers))
     remote(tokens.at[other_rows, :], tok.at[tp, :, own_feat], send_sem.at[0], tok_sem.at[CHUNKS], sibling).start()
     wait_bytes(own_weight(2), local_sem.at[3])
-    remote(own_weight(2), own_weight(2), send_sem.at[1], w_sem.at[2], sibling).start()
+    for k in range(2):
+        piece = w_in.at[lax.rem(z + 2, 4), own_feat, pl.ds(k * QKV, QKV)]
+        remote(piece, piece, send_sem.at[1], w_sem.at[2 + 2 * k], sibling).start()
     wait_bytes(tok.at[0, :, pl.ds(0, FEATURES)], local_sem.at[0])
     wait_bytes(tok.at[0, :, pl.ds(0, FEATURES)], tok_sem.at[CHUNKS])
     for peer in (y_near, x_next, x_prev):
@@ -243,10 +245,9 @@
         ).start()
         remote(tok.at[after, lower], tok.at[after, lower], send_sem.at[0], far_sem.at[far, 1], x_prev).start()
 
-    def multiply(jc, r):
+    def multiply(jc, r, cols=pl.ds(0, 2 * QKV)):
         zi = lax.rem(z + r, 4)
-
-        part[jc, r] = jnp.dot(tok[jc], w_in[zi], preferred_element_type=F32).astype(BF16)
+        part[jc, r, :, cols] = jnp.dot(tok[jc], w_in[zi, :, cols], preferred_element_type=F32).astype(BF16)
 
     first, second = pl.ds(0, QKV), pl.ds(QKV, QKV)
 
@@ -262,17 +263,23 @@
         jc = order(i)
         await_tokens(jc)
 
-        for r in (2, 1, 3, 0):
+        for k, cols, peer in ((0, first, z_next), (1, second, z_prev)):
+
+            @pl.when(i == 0)
+            def _():
+                wait_bytes(w_in.at[0, other_feat, cols], w_sem.at[2 + 2 * k])
+
+            multiply(jc, 2, cols)
+            remote(part.at[jc, 2, :, cols], relay.at[k, jc], send_sem.at[2], relay_sem.at[k, jc], peer).start()
+
+        for r in (1, 3, 0):
 
             @pl.when(i == 0)
             def _():
                 wait_bytes(w_in.at[0, other_feat, :], w_sem.at[r])
 
             multiply(jc, r)
-            if r == 2:
-                remote(part.at[jc, 2, :, first], relay.at[0, jc], send_sem.at[2], relay_sem.at[0, jc], z_next).start()
-                remote(part.at[jc, 2, :, second], relay.at[1, jc], send_sem.at[2], relay_sem.at[1, jc], z_prev).start()
-            elif r == 1:
+            if r == 1:
                 remote(part.at[jc, 1, :, second], direct.at[1, jc], send_sem.at[3], direct_sem.at[1, jc], z_next).start()
             elif r == 3:
                 remote(part.at[jc, 3, :, first], direct.at[0, jc], send_sem.at[3], direct_sem.at[0, jc], z_prev).start()
@@ -690,7 +697,7 @@
         dma((9,)),
         dma((CHUNKS + 1,)),
         dma((2, 2)),
-        dma((4,)),
+        dma((5,)),
         dma((1,)),
         dma((2, CHUNKS)),
         dma((2, CHUNKS)),

time: 99.7 us -> 99.6 us (level)
  no operation moved by 1% of the time
where the time goes in v9:
time: 99.6 us; the launch traced here: 99.5 us
  Pallas kernels  98.7 us (99%)
    pallas_call x1, Pallas kernels, local(): pl.pallas_call(kernel, out_shape=pltpu.VMEM(tokens.shape, BF16), in_specs...  98.7 us

profile of v9, /device:TPU:15, one launch (start us, length us, event | category | flops | bytes accessed | tf_op | source)
XLA Modules:
  0.0 99.5 jit_solution(2879323350754539276)
XLA Ops:
  0.0 98.7 %hyena_block.1 = bf16[256,512]{1,0:T(8,128)(2,1)S(1)} custom-call(bf16[256,512]{1,0:T(8,128)(2,1)} %tokens.1, bf16[3,512,1024]{2,1,0:T(8,128)(2,1)} %bitcast.2, f32[16,1024]{1,0:T(8,128)} %residues_in.1, f32[16,1024]{1,0:T(8,128)} %decay_rates_in.1, f32[1,1024]{1,0:T(1,128)} %bitcast.3, bf16[1024,512]{1,0:T(8,128)(2,1)} %out_weight.1), custom_call_target="tpu_custom_call" | custom-call | tf_op jit(solution)/shard_map/hyena_block/pallas_call | solution.py:719
  98.8 0.7 copy.8
